TPU v7x, 32 devices: a whole 2x2x4 slice. The times are simulated.
32 devices in a mesh: parts: 2 (over x), frame: 8 (over z, y), clip: 2 (over core).
Axes of the slice: x: 2, y: 2, z: 4, core: 2. Of those that a mesh axis runs over, the one named last changes fastest.
Arguments:
- activations: bfloat16 [4, 8, 384, 384], P(('parts', 'clip'), 'frame'), parts along dimension 0, may hold values from -6 to 6
- cotangent: bfloat16 [4, 8, 384, 384], P(('parts', 'clip'), 'frame'), parts along dimension 0, may hold values from -37 to 37
- norm_gains: float32 [3, 384], replicated, may hold values from 0.1 to 1.9
- time_input: bfloat16 [384, 1152], replicated, may hold values from -4 to 4, as said below
- time_output: bfloat16 [384, 384], replicated, may hold values from -0.3125 to 0.3125
- space_input: bfloat16 [384, 1152], replicated, may hold values from -4 to 4, as said below
- space_output: bfloat16 [384, 384], replicated, may hold values from -0.3125 to 0.3125
- hidden_up: bfloat16 [384, 1536], replicated, may hold values from -0.3125 to 0.3125
- hidden_down: bfloat16 [1536, 384], replicated, may hold values from -0.15625 to 0.15625
Outputs:
- input_grad: bfloat16 [4, 8, 384, 384], P(('parts', 'clip'), 'frame'), parts along dimension 0
- time_input_grad: float32 [768, 1152], P(('parts', 'frame')), parts along dimension 0
- time_output_grad: float32 [768, 384], P(('parts', 'frame')), parts along dimension 0
- space_input_grad: float32 [768, 1152], P(('parts', 'frame')), parts along dimension 0
- space_output_grad: float32 [768, 384], P(('parts', 'frame')), parts along dimension 0
- hidden_up_grad: float32 [768, 1536], P(('parts', 'frame')), parts along dimension 0
- hidden_down_grad: float32 [3072, 384], P(('parts', 'frame')), parts along dimension 0
- norm_gains_grad: float32 [6, 384], P('parts'), parts along dimension 0
There are 2 independent parts, one for each index of `parts`. A program takes and returns all parts, laid end to end along the dimension named above; an argument that names none is the same for every part. Nothing has to cross between parts.
Inputs may be any that keep to these rules, and one draw needn't show every extreme that they name: `time_input`: a real-valued projection matrix. `space_input`: a real-valued projection matrix.
All inputs are finite; a program needn't handle non-finite values.
Results may differ from a plain program's by a relative error of at most 0.025.
Values may be sent and summed in bfloat16 or wider, within the bound.
No kernel may reach another device: no remote copies, remote signals or barrier semaphores. Data moves between devices by JAX's collectives and lax.ppermute only.
A program may use at most 128 MiB of HBM per device.

v0:
```python
import jax
import jax.numpy as jnp
from jax import lax
from jax.sharding import PartitionSpec as P

HEADS = 6


epsilon = 1e-06


def contract(form, left_op, right_op):
    return jnp.einsum(form, left_op, right_op, preferred_element_type=jnp.float32)


def normalize(wide_rows, gain):
    center = jnp.mean(wide_rows, axis=-1, keepdims=True)
    offset = wide_rows - center
    inverse = lax.rsqrt(jnp.mean(offset * offset, axis=-1, keepdims=True) + epsilon)
    normed = offset * inverse
    return ((normed * gain).astype(jnp.bfloat16), normed, inverse)


def normalize_back(hidden_grad, normed, inverse, gain):
    scaled = hidden_grad * gain
    return inverse * (
        scaled
        - jnp.mean(scaled, axis=-1, keepdims=True)
        - normed * jnp.mean(scaled * normed, axis=-1, keepdims=True)
    )


def times_weight(left_rows, weight):
    flat = left_rows.reshape(-1, left_rows.shape[-1])
    result = jnp.dot(flat, weight, preferred_element_type=jnp.float32)
    return result.reshape(left_rows.shape[:-1] + (weight.shape[1],))


def times_transposed(left_rows, weight):
    flat = left_rows.reshape(-1, left_rows.shape[-1])
    result = lax.dot_general(
        flat, weight, (((1,), (1,)), ((), ())), preferred_element_type=jnp.float32
    )
    return result.reshape(left_rows.shape[:-1] + (weight.shape[0],))


def outer_sum(left_rows, right_rows):
    return lax.dot_general(
        left_rows, right_rows, (((0,), (0,)), ((), ())), preferred_element_type=jnp.float32
    )


def attention_forms(seq_first):
    if seq_first:
        return ("qbhe,kbhe->bhqk", "bhqk,kbhe->qbhe", "bhqk,qbhe->kbhe")
    return ("bqhe,bkhe->bhqk", "bhqk,bkhe->bqhe", "bhqk,bqhe->bkhe")


def split_heads(packed):
    grouped = packed.reshape(packed.shape[:-1] + (3, HEADS, packed.shape[-1] // (3 * HEADS)))
    return (grouped[..., 0, :, :], grouped[..., 1, :, :], grouped[..., 2, :, :])


def attention_shares(queries, key_rows, seq_first):
    factor = queries.shape[-1] ** (-0.5)
    scores = contract(attention_forms(seq_first)[0], queries, key_rows) * factor
    scores = scores - jnp.max(scores, axis=-1, keepdims=True)
    raised = jnp.exp(scores)
    return raised / jnp.sum(raised, axis=-1, keepdims=True)


def attend(packed, seq_first):
    queries, key_rows, value_rows = split_heads(packed)
    shares = attention_shares(queries, key_rows, seq_first)
    mixed = contract(attention_forms(seq_first)[1], shares.astype(jnp.bfloat16), value_rows).astype(
        jnp.bfloat16
    )
    return mixed.reshape(mixed.shape[:-2] + (-1,))


def attend_back(packed, mixed_grad, seq_first):
    score_form, out_form, back_form = attention_forms(seq_first)
    queries, key_rows, value_rows = split_heads(packed)
    grad_heads = mixed_grad.reshape(queries.shape)
    shares = attention_shares(queries, key_rows, seq_first)
    share_grad = contract(score_form, grad_heads, value_rows)
    value_grad = contract(back_form, shares.astype(jnp.bfloat16), grad_heads).astype(jnp.bfloat16)
    score_grad = shares * (share_grad - jnp.sum(share_grad * shares, axis=-1, keepdims=True))
    score_low = (score_grad * queries.shape[-1] ** (-0.5)).astype(jnp.bfloat16)
    query_grad = contract(out_form, score_low, key_rows).astype(jnp.bfloat16)
    key_grad = contract(back_form, score_low, queries).astype(jnp.bfloat16)
    stacked = jnp.stack([query_grad, key_grad, value_grad], axis=-3)
    return stacked.reshape(stacked.shape[:-3] + (-1,))


def attention_layer(rows_in, gain, in_proj, out_proj):
    wide_rows = rows_in.astype(jnp.float32)
    hidden, normed, inverse = normalize(wide_rows, gain)
    packed = times_weight(hidden, in_proj).astype(jnp.bfloat16)
    mixed = attend(packed, False)
    rows_out = (wide_rows + times_weight(mixed, out_proj)).astype(jnp.bfloat16)
    return (rows_out, (hidden, normed, inverse, packed, mixed))


def input_back(rows_grad, packed_grad, normed, inverse, gain, in_proj):
    hidden_grad = times_transposed(packed_grad, in_proj)
    gain_term = jnp.sum((hidden_grad * normed).reshape(-1, hidden_grad.shape[-1]), axis=0)
    grad_in = (
        rows_grad.astype(jnp.float32) + normalize_back(hidden_grad, normed, inverse, gain)
    ).astype(jnp.bfloat16)
    return (grad_in, gain_term)


def mlp_forward(rows_in, gain, up_proj):
    hidden, normed, inverse = normalize(rows_in.astype(jnp.float32), gain)
    before = times_weight(hidden, up_proj)
    active = jax.nn.gelu(before).astype(jnp.bfloat16)
    return (hidden, normed, inverse, before, active)


def mlp_back(rows_grad, saved, gain, up_proj, down_proj):
    hidden, normed, inverse, before, active = saved
    active_grad = times_transposed(rows_grad, down_proj)
    before_grad = jax.vjp(jax.nn.gelu, before)[1](active_grad)[0].astype(jnp.bfloat16)
    hidden_grad = times_transposed(before_grad, up_proj)
    gain_term = jnp.sum(hidden_grad * normed, axis=0)
    grad_in = (
        rows_grad.astype(jnp.float32) + normalize_back(hidden_grad, normed, inverse, gain)
    ).astype(jnp.bfloat16)
    return (grad_in, before_grad, gain_term)


def reduce_pairs(grad_pairs, factor):
    shards = []
    for left_rows, right_rows in grad_pairs:
        left_flat = left_rows.reshape(-1, left_rows.shape[-1])
        right_flat = right_rows.reshape(-1, right_rows.shape[-1])

        def grad_term(first_row, row_count, left_flat=left_flat, right_flat=right_flat):
            return outer_sum(left_flat, right_flat) * factor

        row_share = left_flat.shape[1] // lax.axis_size("frame")
        shards.append(
            lax.psum_scatter(
                grad_term(jnp.int32(0), lax.axis_size("frame") * row_share),
                "frame",
                scatter_dimension=0,
                tiled=True,
            )
        )
    return (
        lax.psum(shards[0].astype(jnp.bfloat16), "clip").astype(jnp.float32),
        lax.psum(shards[1].astype(jnp.bfloat16), "clip").astype(jnp.float32),
    )


def body(
    activations,
    cotangent,
    norm_gains,
    time_input,
    time_output,
    space_input,
    space_output,
    hidden_up,
    hidden_down,
):
    local_frames = activations.shape[1]
    patches = activations.shape[2]
    model_width = activations.shape[3]
    frame_count = lax.axis_size("frame")
    patch_share = patches // frame_count
    tokens_all = activations.shape[0] * lax.axis_size("clip") * local_frames * frame_count * patches
    factor = tokens_all ** (-0.5)
    frame_rows = activations.reshape(local_frames, patches, model_width)
    wide_rows = frame_rows.astype(jnp.float32)
    time_hidden, time_normed, time_inverse = normalize(wide_rows, norm_gains[0])
    time_packed = times_weight(time_hidden, time_input).astype(jnp.bfloat16)
    section = lax.all_to_all(
        time_packed.reshape(local_frames, frame_count, patch_share, -1),
        "frame",
        split_axis=1,
        concat_axis=0,
        tiled=True,
    )
    mixed = attend(section[:, 0], True)
    mixed_patch = mixed[:, None]
    time_mixed = lax.all_to_all(
        mixed_patch, "frame", split_axis=0, concat_axis=1, tiled=True
    ).reshape(local_frames, patches, model_width)
    first_out = (wide_rows + times_weight(time_mixed, time_output)).astype(jnp.bfloat16)
    second_out, space_saved = attention_layer(first_out, norm_gains[1], space_input, space_output)
    flat_rows = second_out.reshape(-1, model_width)
    mlp_saved = mlp_forward(flat_rows, norm_gains[2], hidden_up)
    flat_grad = cotangent.reshape(-1, model_width)
    second_grad, before_grad, third_gain = mlp_back(
        flat_grad, mlp_saved, norm_gains[2], hidden_up, hidden_down
    )
    down_grad, up_grad = reduce_pairs(
        ((mlp_saved[4], flat_grad), (mlp_saved[0], before_grad)), factor
    )
    second_rows = second_grad.reshape(local_frames, patches, model_width)
    space_hidden, space_normed, space_inverse, space_packed, space_mixed = space_saved
    space_mixed_grad = times_transposed(second_rows, space_output).astype(jnp.bfloat16)
    space_packed_grad = attend_back(space_packed, space_mixed_grad, False)
    first_grad, second_gain = input_back(
        second_rows, space_packed_grad, space_normed, space_inverse, norm_gains[1], space_input
    )
    space_output_grad, space_input_grad = reduce_pairs(
        ((space_mixed, second_rows), (space_hidden, space_packed_grad)), factor
    )
    time_mixed_grad = times_transposed(first_grad, time_output).astype(jnp.bfloat16)
    patch_grad = lax.all_to_all(
        time_mixed_grad.reshape(local_frames, frame_count, patch_share, model_width),
        "frame",
        split_axis=1,
        concat_axis=0,
        tiled=True,
    )
    packed_patch_grad = attend_back(section[:, 0], patch_grad[:, 0], True)
    time_packed_grad = lax.all_to_all(
        packed_patch_grad[:, None], "frame", split_axis=0, concat_axis=1, tiled=True
    ).reshape(local_frames, patches, -1)
    input_rows, first_gain = input_back(
        first_grad, time_packed_grad, time_normed, time_inverse, norm_gains[0], time_input
    )
    time_output_grad, time_input_grad = reduce_pairs(
        ((time_mixed, first_grad), (time_hidden, time_packed_grad)), factor
    )
    norm_gains_grad = lax.psum(
        jnp.stack([first_gain, second_gain, third_gain]) * factor, ("frame", "clip")
    )
    return (
        input_rows.reshape(activations.shape),
        time_input_grad,
        time_output_grad,
        space_input_grad,
        space_output_grad,
        up_grad,
        down_grad,
        norm_gains_grad,
    )


def solution(mesh):
    in_specs = (
        P(("parts", "clip"), "frame", None, None),
        P(("parts", "clip"), "frame", None, None),
        P(),
        P(),
        P(),
        P(),
        P(),
        P(),
        P(),
    )
    out_specs = (
        P(("parts", "clip"), "frame", None, None),
        P(("parts", "frame"), None),
        P(("parts", "frame"), None),
        P(("parts", "frame"), None),
        P(("parts", "frame"), None),
        P(("parts", "frame"), None),
        P(("parts", "frame"), None),
        P("parts", None),
    )
    return jax.shard_map(body, mesh=mesh, in_specs=in_specs, out_specs=out_specs, check_vma=False)
```

profile of v0, /device:TPU:0, one launch (start us, length us, event | category | flops | bytes accessed | tf_op | source)
XLA Modules:
  0.0 588.4 jit_solution(4909259870669012119)
XLA Ops:
  11.4 29.8 %all_to_all.16 = bf16[1,8,48,1152]{3,2,0,1:T(8,128)(2,1)S(1)} all-to-all(bf16[1,8,48,1152]{3,2,0,1:T(8,128)(2,1)S(1)} %bitcast.210), channel_id=1, replica_groups=mesh['parts'=2,'frame'=8,'clip'=2] {'frame'}, dimensions={1} | all-to-all | bytes 1769472 | tf_op jit(solution)/shard_map/all_to_all | solution.py:179
  41.2 2.6 reshape_squeeze.7
  43.9 3.0 fusion.123
  46.9 3.9 fusion.124
  54.1 3.4 all-to-all-start.1
  59.6 7.0 %all-to-all-done.1 = bf16[8,1,48,384]{3,2,1,0:T(8,128)(2,1)S(1)} async-done(((bf16[8,1,48,384]{3,2,1,0:T(8,128)(2,1)}), bf16[8,1,48,384]{3,2,1,0:T(8,128)(2,1)S(1)}, u32[]{:S(2)}, u32[]{:S(2)}) %all-to-all-start.1) | async-done | bytes 294944 | tf_op jit(solution)/shard_map/all_to_all | solution.py:188
  67.2 2.9 convolution_convert_fusion
  70.0 2.2 copy.55
  72.2 4.0 fusion.126
  76.2 2.5 convolution_convert_fusion.7
  86.8 3.5 fusion.56
  90.2 3.4 fusion.105
  93.7 7.0 %fusion.53 = bf16[1,384,1,6,64]{1,4,3,2,0:T(8,128)(2,1)} fusion(f32[6,384,384]{1,2,0:T(8,128)} %fusion.105, bf16[1,384,3,6,64]{1,4,3,2,0:T(8,128)(2,1)} %bitcast.203, f32[6,384,384]{1,2,0:T(8,128)} %get-tuple-element.58, f32[6,384]{1,0:T(8,128)} %copy-done.32), kind=kOutput, calls=%fused_computation.67 | convolution fusion | flops 119589504 | bytes 14770176 | tf_op jit(solution)/shard_map/bhqk,bkhe->bqhe/dot_general | solution.py:13
  100.7 7.1 %fusion.50 = bf16[1,384,1,6,64]{1,4,3,2,0:T(8,128)(2,1)} fusion(f32[6,384,384]{1,2,0:T(8,128)} %fusion.105, bf16[1,384,3,6,64]{1,4,3,2,0:T(8,128)(2,1)} %bitcast.204, f32[6,384,384]{1,2,0:T(8,128)} %get-tuple-element.58, f32[6,384]{1,0:T(8,128)} %copy-done.32), kind=kOutput, calls=%fused_computation.66 | convolution fusion | flops 119589504 | bytes 14770176 | tf_op jit(solution)/shard_map/bhqk,bqhe->bkhe/dot_general | solution.py:13
  109.1 2.9 multiply_reduce_fusion.4
  113.5 55.7 %reduce-scatter.13.cloned.1.call-done = f32[48,384]{1,0:T(8,128)} async-done(((f32[384,384]{1,0:T(8,128)}), f32[48,384]{1,0:T(8,128)}) %reduce-scatter.13.cloned.1.call-update) | async-done | bytes 73744 | tf_op jit(solution)/shard_map/reduce_scatter | solution.py:144
  170.7 63.3 %reduce-scatter.9.cloned.1.call-done = f32[48,384]{1,0:T(8,128)} async-done(((f32[384,384]{1,0:T(8,128)}), f32[48,384]{1,0:T(8,128)}) %reduce-scatter.9.cloned.1.call-update) | async-done | bytes 73744 | tf_op jit(solution)/shard_map/reduce_scatter | solution.py:144
  235.8 3.1 convolution_multiply_fusion
  239.0 4.2 convolution_multiply_fusion.2
  243.9 3.5 convolution_multiply_fusion.3
  247.8 12.4 %all_to_all.17 = bf16[1,8,48,384]{3,2,0,1:T(8,128)(2,1)} all-to-all(bf16[1,8,48,384]{3,2,0,1:T(8,128)(2,1)S(1)} %bitcast.207), channel_id=1, replica_groups=mesh['parts'=2,'frame'=8,'clip'=2] {'frame'}, dimensions={1} | all-to-all | bytes 589824 | tf_op jit(solution)/shard_map/all_to_all | solution.py:213
  263.6 4.6 fusion.33
  268.2 4.1 fusion.34
  272.3 2.0 fusion.35
  276.6 3.3 broadcast_in_dim_reshape.7
  279.9 26.2 %all_to_all.18 = bf16[8,1,48,1152]{3,2,1,0:T(8,128)(2,1)S(1)} all-to-all(bf16[8,1,48,1152]{3,2,1,0:T(8,128)(2,1)S(1)} %bitcast.197), channel_id=1, replica_groups=mesh['parts'=2,'frame'=8,'clip'=2] {'frame'}, dimensions={0} | all-to-all | bytes 1769472 | tf_op jit(solution)/shard_map/all_to_all | solution.py:221
  311.0 2.0 fusion.72
  313.0 15.5 %reduce-scatter.11.cloned.1.call-done = f32[48,1152]{1,0:T(8,128)} async-done(((f32[384,1152]{1,0:T(8,128)}), f32[48,1152]{1,0:T(8,128)}) %reduce-scatter.11.cloned.1.call-update) | async-done | bytes 221200 | tf_op jit(solution)/shard_map/reduce_scatter | solution.py:144
  330.0 70.6 %reduce-scatter.17.cloned.1.call-done = f32[192,384]{1,0:T(8,128)} async-done(((f32[1536,384]{1,0:T(8,128)}), f32[192,384]{1,0:T(8,128)}) %reduce-scatter.17.cloned.1.call-update) | async-done | bytes 294928 | tf_op jit(solution)/shard_map/reduce_scatter | solution.py:144
  402.2 70.3 %reduce-scatter.15.cloned.1.call-done = f32[48,1536]{1,0:T(8,128)} async-done(((f32[384,1536]{1,0:T(8,128)}), f32[48,1536]{1,0:T(8,128)}) %reduce-scatter.15.cloned.1.call-update) | async-done | bytes 294928 | tf_op jit(solution)/shard_map/reduce_scatter | solution.py:144
  474.1 67.3 %reduce-scatter.7.cloned.1.call-done = f32[48,1152]{1,0:T(8,128)} async-done(((f32[384,1152]{1,0:T(8,128)}), f32[48,1152]{1,0:T(8,128)}) %reduce-scatter.7.cloned.1.call-update) | async-done | bytes 221200 | tf_op jit(solution)/shard_map/reduce_scatter | solution.py:144
  544.2 30.9 %psum.55 = f32[3,384]{1,0:T(4,128)} all-reduce(f32[3,384]{1,0:T(4,128)S(1)} %maximum_multiply_fusion), channel_id=1, replica_groups=mesh['parts'=2,'frame'=8,'clip'=2] {'frame','clip'}, use_global_device_ids=true, to_apply=%region_33.0 | all-reduce | flops 1152 | bytes 9216 | tf_op jit(solution)/shard_map/psum | solution.py:230
  (141 shorter events, 49.8 us)
Async XLA Ops:
  7.2 72.2 %copy-start = (bf16[384,1536]{1,0:T(8,128)(2,1)S(1)}, bf16[384,1536]{1,0:T(8,128)(2,1)}, u32[]{:S(2)}) copy-start(bf16[384,1536]{1,0:T(8,128)(2,1)} %param.16) | copy-start | bytes 3538948
  8.0 33.2 %copy-start.25 = (f32[384]{0:T(512)}, f32[384]{0:T(512)S(1)}, u32[]{:S(2)}) copy-start(f32[384]{0:T(512)S(1)} %get-tuple-element.42) | copy-start | bytes 4612
  8.0 59.1 %copy-start.19 = (f32[384]{0:T(512)}, f32[384]{0:T(512)S(1)}, u32[]{:S(2)}) copy-start(f32[384]{0:T(512)S(1)} %get-tuple-element.43) | copy-start | bytes 4612
  9.4 34.4 %copy-start.23 = (f32[384]{0:T(512)}, f32[384]{0:T(512)S(1)}, u32[]{:S(2)}) copy-start(f32[384]{0:T(512)S(1)} %add_rsqrt_fusion.2) | copy-start | bytes 4612
  46.8 3.9 copy-start.2
  46.8 5.9 %copy-start.10 = (bf16[8,48,1,6,64]{4,3,2,1,0:T(8,128)(2,1)}, bf16[8,48,1,6,64]{4,3,2,1,0:T(8,128)(2,1)S(1)}, u32[]{:S(2)}) copy-start(bf16[8,48,1,6,64]{4,3,2,1,0:T(8,128)(2,1)S(1)} %get-tuple-element.51) | copy-start | bytes 884740
  52.8 13.9 %copy-start.6 = (bf16[384,384]{1,0:T(8,128)(2,1)S(1)}, bf16[384,384]{1,0:T(8,128)(2,1)}, u32[]{:S(2)}) copy-start(bf16[384,384]{1,0:T(8,128)(2,1)} %param.13) | copy-start | bytes 884740
  54.1 12.5 %all-to-all-start.1 = ((bf16[8,1,48,384]{3,2,1,0:T(8,128)(2,1)}), bf16[8,1,48,384]{3,2,1,0:T(8,128)(2,1)S(1)}, u32[]{:S(2)}, u32[]{:S(2)}) async-start(bf16[8,1,48,384]{3,2,1,0:T(8,128)(2,1)} %bitcast.9), calls=%async_computation.1 | async-start | bytes 589824 | tf_op jit(solution)/shard_map/all_to_all | solution.py:188
  57.6 111.6 %reduce-scatter.13.cloned.1.call-start = ((), (), s32[]{:S(2)}) async-start(), calls=%async_computation.13 | async-start | bytes 663552 | tf_op jit(solution)/shard_map/reduce_scatter | solution.py:144
  67.1 9.1 %copy-start.21 = (f32[384]{0:T(512)}, f32[384]{0:T(512)S(1)}, u32[]{:S(2)}) copy-start(f32[384]{0:T(512)S(1)} %add_rsqrt_fusion.1) | copy-start | bytes 4612
  76.2 2.6 copy-start.32
  76.2 2.6 copy-start.5
  79.4 4.7 copy-start.17
  100.7 7.2 %copy-start.14 = (bf16[1,384,1,6,64]{1,4,3,2,0:T(8,128)(2,1)S(1)}, bf16[1,384,1,6,64]{1,4,3,2,0:T(8,128)(2,1)}, u32[]{:S(2)}) copy-start(bf16[1,384,1,6,64]{1,4,3,2,0:T(8,128)(2,1)} %fusion.56) | copy-start | bytes 884740
  107.8 126.2 %reduce-scatter.9.cloned.1.call-start = ((), (), s32[]{:S(2)}) async-start(), calls=%async_computation.11 | async-start | bytes 663552 | tf_op jit(solution)/shard_map/reduce_scatter | solution.py:144
  107.9 4.1 copy-start.20
  107.9 4.1 copy-start.22
  109.1 3.1 copy-start.1
  113.4 194.7 %all-reduce.5.cloned.1.call-start = ((), (), s32[]{:S(2)}) async-start(), calls=%async_computation.16 | async-start | bytes 147456 | tf_op jit(solution)/shard_map/psum | solution.py:152
  235.5 3.5 copy-start.16
  235.5 92.9 %reduce-scatter.11.cloned.1.call-start = ((), (), s32[]{:S(2)}) async-start(), calls=%async_computation.12 | async-start | bytes 1990656 | tf_op jit(solution)/shard_map/reduce_scatter | solution.py:144
  239.0 161.6 %reduce-scatter.17.cloned.1.call-start = ((), (), s32[]{:S(2)}) async-start(), calls=%async_computation.15 | async-start | bytes 2654208 | tf_op jit(solution)/shard_map/reduce_scatter | solution.py:144
  243.3 4.2 copy-start.7
  243.3 229.2 %reduce-scatter.15.cloned.1.call-start = ((), (), s32[]{:S(2)}) async-start(), calls=%async_computation.14 | async-start | bytes 2654208 | tf_op jit(solution)/shard_map/reduce_scatter | solution.py:144
  247.3 14.4 %copy-start.3 = (bf16[8,48,1,6,64]{4,3,2,1,0:T(8,128)(2,1)S(1)}, bf16[8,48,1,6,64]{4,3,2,1,0:T(8,128)(2,1)}, u32[]{:S(2)}) copy-start(bf16[8,48,1,6,64]{4,3,2,1,0:T(8,128)(2,1)} %copy-done.2) | copy-start | bytes 884740
  247.4 16.2 %copy-start.31 = (f32[48,6,8]{2,1,0:T(8,128)S(1)}, f32[48,6,8]{2,1,0:T(8,128)}, u32[]{:S(2)}) copy-start(f32[48,6,8]{2,1,0:T(8,128)} %copy-done.30) | copy-start | bytes 27652
  247.4 294.0 %reduce-scatter.7.cloned.1.call-start = ((), (), s32[]{:S(2)}) async-start(), calls=%async_computation.10 | async-start | bytes 1990656 | tf_op jit(solution)/shard_map/reduce_scatter | solution.py:144
  263.6 4.6 copy-start.11
  276.6 29.5 %copy-start.24 = (f32[384]{0:T(512)S(1)}, f32[384]{0:T(512)}, u32[]{:S(2)}) copy-start(f32[384]{0:T(512)} %copy-done.23) | copy-start | bytes 4612
  276.6 29.5 %copy-start.26 = (f32[384]{0:T(512)S(1)}, f32[384]{0:T(512)}, u32[]{:S(2)}) copy-start(f32[384]{0:T(512)} %copy-done.25) | copy-start | bytes 4612
  306.1 2.0 copy-start.28
  308.0 267.0 %all-reduce.7.cloned.1.call-start = ((), (), s32[]{:S(2)}) async-start(), calls=%async_computation.17 | async-start | bytes 1032192 | tf_op jit(solution)/shard_map/psum | solution.py:153
  (10 other events, 16.0 us)
Sparse Core Ops, SparseCore 0:
  107.9 61.1 reduce-scatter.12
  172.8 61.1 reduce-scatter.8
  236.9 16.7 all-reduce.4
  257.1 71.3 reduce-scatter.10
  332.2 68.3 reduce-scatter.16
  404.3 68.1 reduce-scatter.14
  476.4 64.9 reduce-scatter.6
  544.5 17.6 all-reduce.6
where the time goes:
time: 590 us; the launch traced here: 588 us
  waiting for transfers between devices  350 us (59%)
  blocking collectives  99.2 us (17%)
  matrix products  77.5 us (13%)
  local copies, waits for them, and re-layouts  21.7 us (4%)
  other arithmetic  21.5 us (4%)
  between operations  14.6 us (2%)
    reduce_scatter x6, waiting for transfers between devices, reduce_pairs(): lax.psum_scatter(grad_term(jnp.int32(0), lax.axis_size('frame') * row_sha...  343 us
    dot_general x10, matrix products, contract(): jnp.einsum(form, left_op, right_op, preferred_element_type=jnp.float32)  38 us
    psum x1, blocking collectives, body(): lax.psum(jnp.stack([first_gain, second_gain, third_gain]) * factor, ('fra...  30.9 us
    all_to_all x1, blocking collectives, body(): lax.all_to_all(time_packed.reshape(local_frames, frame_count, patch_share...  29.8 us
    all_to_all x1, blocking collectives, body(): lax.all_to_all(packed_patch_grad[:, None], 'frame', split_axis=0, concat_...  26.2 us
    dot_general x6, matrix products, outer_sum(): lax.dot_general(left_rows, right_rows, (((0,), (0,)), ((), ())), preferre...  15.2 us
    all_to_all x1, blocking collectives, body(): lax.all_to_all(time_mixed_grad.reshape(local_frames, frame_count, patch_s...  12.4 us
  transfers between devices with their start and end apart: 9, of which 7 were waited for; matrix products, arithmetic and copies ran while one was open for 9% of the time, Pallas kernels for 0%

commit v1 on v0

v1 whole, which is shorter than its diff:
```python
import functools

import jax
import jax.numpy as jnp
from jax import lax
from jax.experimental import pallas as pl
from jax.experimental.pallas import tpu as pltpu
from jax.sharding import PartitionSpec as P

HEADS = 6
HEAD_DIM = 64
SCALE = HEAD_DIM ** (-0.5)
EPSILON = 1e-06
GELU_C = 0.7978845608028654
GELU_A = 0.044715
MASKED = -1e30
F32 = jnp.float32
BF16 = jnp.bfloat16


def nn(a, b):
    return lax.dot_general(a, b, (((1,), (0,)), ((), ())), preferred_element_type=F32)


def nt(a, b):
    return lax.dot_general(a, b, (((1,), (1,)), ((), ())), preferred_element_type=F32)


def tn(a, b):
    return lax.dot_general(a, b, (((0,), (0,)), ((), ())), preferred_element_type=F32)


def normalize(rows):
    offset = rows - jnp.mean(rows, axis=-1, keepdims=True)
    inverse = lax.rsqrt(jnp.mean(offset * offset, axis=-1, keepdims=True) + EPSILON)
    return offset * inverse, inverse


def normalize_back(hidden_grad, normed, inverse, gain):
    scaled = hidden_grad * gain
    return inverse * (
        scaled
        - jnp.mean(scaled, axis=-1, keepdims=True)
        - normed * jnp.mean(scaled * normed, axis=-1, keepdims=True)
    )


def lane_masks(dtype):
    lane = lax.broadcasted_iota(jnp.int32, (1, 2 * HEAD_DIM), 1)
    first = (lane < HEAD_DIM).astype(F32)
    return first.astype(dtype), (1.0 - first).astype(dtype)


def both_heads(pair):
    first, second = lane_masks(pair.dtype)
    return jnp.concatenate([pair * first, pair * second], axis=0)


def merge_heads(stacked):
    first, second = lane_masks(stacked.dtype)
    count = stacked.shape[0] // 2
    return stacked[:count] * first + stacked[count:] * second


def pair_shares(queries, keys_both, mask):
    scores = nt(queries * jnp.asarray(SCALE, BF16), keys_both)
    count = keys_both.shape[0] // 2
    shares = []
    for half in (scores[:, :count], scores[:, count:]):
        if mask is not None:
            half = jnp.where(mask, half, MASKED)
        raised = jnp.exp(half - jnp.max(half, axis=-1, keepdims=True))
        shares.append(raised * (1.0 / jnp.sum(raised, axis=-1, keepdims=True)))
    return shares


def pair_attend(queries, keys, values, mask):
    shares = pair_shares(queries, both_heads(keys), mask)
    return nn(jnp.concatenate([s.astype(BF16) for s in shares], axis=1), both_heads(values))


def pair_attend_back(queries, keys, values, mixed_grad, mask):
    keys_both = both_heads(keys)
    shares = pair_shares(queries, keys_both, mask)
    share_grad = nt(mixed_grad, both_heads(values))
    count = keys.shape[0]
    score_grads = []
    for share, grad in zip(shares, (share_grad[:, :count], share_grad[:, count:])):
        row = jnp.sum(grad * share, axis=-1, keepdims=True)
        score_grads.append((share * (grad - row) * SCALE).astype(BF16))
    score_low = jnp.concatenate(score_grads, axis=1)
    share_low = jnp.concatenate([s.astype(BF16) for s in shares], axis=1)
    query_grad = nn(score_low, keys_both)
    key_grad = merge_heads(tn(score_low, queries))
    value_grad = merge_heads(tn(share_low, mixed_grad))
    return query_grad.astype(BF16), key_grad.astype(BF16), value_grad.astype(BF16)


class Groups:
    def __init__(self, frames, share):
        self.frames, self.share = frames, share
        self.size = 16 if share % 16 == 0 else share
        self.count = share // self.size

    def mask(self):
        rows = self.frames * self.size
        i = lax.broadcasted_iota(jnp.int32, (rows, rows), 0)
        j = lax.broadcasted_iota(jnp.int32, (rows, rows), 1)
        return lax.rem(i, self.size) == lax.rem(j, self.size)

    def load(self, ref, group, first, width):
        parts = [
            ref[pl.ds(f * self.share + group * self.size, self.size), pl.ds(first, width)]
            for f in range(self.frames)
        ]
        if self.count == 1:
            return ref[:, pl.ds(first, width)]
        return jnp.concatenate(parts, axis=0)

    def store(self, ref, group, first, value):
        if self.count == 1:
            ref[:, pl.ds(first, value.shape[1])] = value
            return
        for f in range(self.frames):
            ref[pl.ds(f * self.share + group * self.size, self.size), pl.ds(first, value.shape[1])] = value[
                f * self.size : (f + 1) * self.size
            ]


def time_forward_kernel(groups, x_ref, gains_ref, in_ref, out_ref, first_ref, hidden_ref, packed_ref, mixed_ref):
    rows = x_ref[...].astype(F32)
    width = rows.shape[1]
    normed, _ = normalize(rows)
    hidden = (normed * gains_ref[0:1, :]).astype(BF16)
    hidden_ref[...] = hidden
    packed_ref[...] = nn(hidden, in_ref[...]).astype(BF16)
    mask = groups.mask()
    for group in range(groups.count):
        for first in range(0, width, 2 * HEAD_DIM):
            q, k, v = (groups.load(packed_ref, group, part * width + first, 2 * HEAD_DIM) for part in range(3))
            groups.store(mixed_ref, group, first, pair_attend(q, k, v, mask).astype(BF16))
    first_ref[...] = (rows + nn(mixed_ref[...], out_ref[...])).astype(BF16)


def store_half(core_ref, half, keep_ref, send_ref, store):
    @pl.when(core_ref[0] == half)
    def _():
        store(keep_ref)

    @pl.when(core_ref[0] != half)
    def _():
        store(send_ref)


def block_place(core_ref, owner, frames, rows, by_parity):
    if not by_parity:
        return owner * rows
    return ((owner % 2) ^ core_ref[1]) * (frames // 2 * rows) + owner // 2 * rows


def pack_columns(core_ref, frames, columns, ref, by_parity):
    share = columns[0].shape[0] // frames
    for owner in range(frames):
        place = block_place(core_ref, owner, frames, share * len(columns), by_parity)
        for index, piece in enumerate(columns):
            start = place + index * share
            if by_parity:
                start = pl.multiple_of(start, share)
            ref[pl.ds(start, share), :] = piece[owner * share : (owner + 1) * share]


def pack_rows(core_ref, frames, tall, ref):
    rows = tall.shape[0] // frames
    for owner in range(frames):
        start = pl.multiple_of(block_place(core_ref, owner, frames, rows, True), rows)
        ref[pl.ds(start, rows), :] = tall[owner * rows : (owner + 1) * rows]


def space_mlp_kernel(
    frames, factor, packed_grads,
    core_ref, x_ref, cot_ref, gains_ref, in_ref, out_ref, up_ref, down_ref,
    grad_ref, hidden_ref, packed_ref, mixed_ref, gain_ref, keep_ref, send_ref,
):
    rows = x_ref[...].astype(F32)
    width = rows.shape[1]
    normed, _ = normalize(rows)
    hidden = (normed * gains_ref[1:2, :]).astype(BF16)
    hidden_ref[...] = hidden
    packed_ref[...] = nn(hidden, in_ref[...]).astype(BF16)
    for first in range(0, width, 2 * HEAD_DIM):
        q, k, v = (packed_ref[:, pl.ds(part * width + first, 2 * HEAD_DIM)] for part in range(3))
        mixed_ref[:, pl.ds(first, 2 * HEAD_DIM)] = pair_attend(q, k, v, None).astype(BF16)
    second = (rows + nn(mixed_ref[...], out_ref[...])).astype(BF16)
    normed, inverse = normalize(second.astype(F32))
    gain = gains_ref[2:3, :]
    mlp_hidden = (normed * gain).astype(BF16)
    before = nn(mlp_hidden, up_ref[...])
    square = before * before
    bent = jnp.tanh(GELU_C * before * (1.0 + GELU_A * square))
    half_bent = 0.5 + 0.5 * bent
    active = (before * half_bent).astype(BF16)
    slope = half_bent + 0.5 * before * (1.0 - bent * bent) * (GELU_C * (1.0 + 3.0 * GELU_A * square))
    cot = cot_ref[...]
    before_grad = (slope * nt(cot, down_ref[...])).astype(BF16)
    hidden_grad = nt(before_grad, up_ref[...])
    gain_ref[...] = jnp.sum(hidden_grad * normed, axis=0, keepdims=True)
    grad_ref[...] = (cot.astype(F32) + normalize_back(hidden_grad, normed, inverse, gain)).astype(BF16)
    up_grad = (tn(mlp_hidden, before_grad) * factor).astype(BF16)
    down_grad = (tn(active, cot) * factor).astype(BF16)
    if packed_grads:
        pieces = [up_grad[:, first : first + width] for first in range(0, up_grad.shape[1], width)]
        store_half(core_ref, 0, keep_ref, send_ref, lambda ref: pack_columns(core_ref, frames, pieces, ref, True))
        store_half(core_ref, 1, keep_ref, send_ref, lambda ref: pack_rows(core_ref, frames, down_grad, ref))
    else:
        keep_ref[...] = up_grad
        send_ref[...] = down_grad


def space_back_kernel(
    x_ref, second_ref, packed_ref, gains_ref, in_ref, out_ref, grad_ref, packed_grad_ref, gain_ref
):
    second = second_ref[...]
    width = second.shape[1]
    mixed_grad = nt(second, out_ref[...]).astype(BF16)
    for first in range(0, width, 2 * HEAD_DIM):
        q, k, v = (packed_ref[:, pl.ds(part * width + first, 2 * HEAD_DIM)] for part in range(3))
        grads = pair_attend_back(q, k, v, mixed_grad[:, first : first + 2 * HEAD_DIM], None)
        for part, grad in enumerate(grads):
            packed_grad_ref[:, pl.ds(part * width + first, 2 * HEAD_DIM)] = grad
    hidden_grad = nt(packed_grad_ref[...], in_ref[...])
    normed, inverse = normalize(x_ref[...].astype(F32))
    gain_ref[...] = jnp.sum(hidden_grad * normed, axis=0, keepdims=True)
    grad_ref[...] = (
        second.astype(F32) + normalize_back(hidden_grad, normed, inverse, gains_ref[1:2, :])
    ).astype(BF16)


def store_attention_grads(core_ref, frames, packed_grads, by_parity, in_grad, out_grad, keep_ref, send_ref):
    width = out_grad.shape[1]
    if packed_grads:
        pieces = [in_grad[:, first : first + width] for first in range(0, in_grad.shape[1], width)] + [out_grad]
        for half in range(2):
            store_half(
                core_ref, half, keep_ref, send_ref,
                lambda ref, half=half: pack_columns(
                    core_ref, frames, pieces[2 * half : 2 * half + 2], ref, by_parity
                ),
            )
    else:
        keep_ref[...] = in_grad
        send_ref[...] = out_grad


def space_weights_kernel(
    frames, factor, packed_grads, core_ref, hidden_ref, packed_grad_ref, mixed_ref, second_ref, keep_ref, send_ref
):
    in_grad = (tn(hidden_ref[...], packed_grad_ref[...]) * factor).astype(BF16)
    out_grad = (tn(mixed_ref[...], second_ref[...]) * factor).astype(BF16)
    store_attention_grads(core_ref, frames, packed_grads, True, in_grad, out_grad, keep_ref, send_ref)


def time_back_kernel(
    groups, factor, packed_grads,
    core_ref, grad_ref, hidden_ref, packed_ref, mixed_ref, out_ref,
    packed_grad_ref, keep_ref, send_ref, mixed_grad_ref,
):
    grad = grad_ref[...]
    width = grad.shape[1]
    mixed_grad_ref[...] = nt(grad, out_ref[...]).astype(BF16)
    mask = groups.mask()
    for group in range(groups.count):
        for first in range(0, width, 2 * HEAD_DIM):
            q, k, v = (groups.load(packed_ref, group, part * width + first, 2 * HEAD_DIM) for part in range(3))
            grads = pair_attend_back(q, k, v, groups.load(mixed_grad_ref, group, first, 2 * HEAD_DIM), mask)
            for part, value in enumerate(grads):
                groups.store(packed_grad_ref, group, part * width + first, value)
    in_grad = (tn(hidden_ref[...], packed_grad_ref[...]) * factor).astype(BF16)
    out_grad = (tn(mixed_ref[...], grad) * factor).astype(BF16)
    store_attention_grads(core_ref, groups.frames, packed_grads, False, in_grad, out_grad, keep_ref, send_ref)


def time_input_kernel(x_ref, grad_ref, packed_grad_ref, gains_ref, in_ref, input_ref, gain_ref):
    hidden_grad = nt(packed_grad_ref[...], in_ref[...])
    normed, inverse = normalize(x_ref[...].astype(F32))
    gain_ref[...] = jnp.sum(hidden_grad * normed, axis=0, keepdims=True)
    input_ref[...] = (
        grad_ref[...].astype(F32) + normalize_back(hidden_grad, normed, inverse, gains_ref[0:1, :])
    ).astype(BF16)


def call(kernel, outs, args, scalars=0, scratch=(), flops=0, name=None):
    vmem = pl.BlockSpec(memory_space=pltpu.VMEM)
    specs = [pl.BlockSpec(memory_space=pltpu.SMEM)] * scalars + [vmem] * (len(args) - scalars)
    return pl.pallas_call(
        kernel,
        out_shape=[jax.ShapeDtypeStruct(shape, dtype) for shape, dtype in outs],
        in_specs=specs,
        out_specs=[vmem] * len(outs),
        scratch_shapes=list(scratch),
        compiler_params=pltpu.CompilerParams(vmem_limit_bytes=40 * 1024 * 1024),
        cost_estimate=pl.CostEstimate(flops=flops, transcendentals=0, bytes_accessed=4000000),
        name=name,
    )(*args)


def natural_halves(core, frames, by_parity, first, second):
    width = min(first.shape[1], second.shape[1])

    def blocks(matrix):
        matrix = matrix.reshape(frames, matrix.shape[0] // frames, -1, width)
        return jnp.swapaxes(matrix, 1, 2).reshape(frames, -1, width)

    first, second = blocks(first), blocks(second)
    if first.shape != second.shape:
        whole = jnp.concatenate([first, second], axis=1)
        middle = whole.shape[1] // 2
        first, second = whole[:, :middle], whole[:, middle:]
    if by_parity:

        def order(blocked):
            blocked = jnp.swapaxes(blocked.reshape((frames // 2, 2) + blocked.shape[1:]), 0, 1)
            return jnp.where(core[1] == 0, blocked, blocked[::-1]).reshape((frames,) + blocked.shape[2:])

        first, second = order(first), order(second)
    swap = core[0] == 0
    return jnp.where(swap, first, second), jnp.where(swap, second, first)


def swap_clips(array):
    return lax.ppermute(array, "clip", [(0, 1), (1, 0)])


def summed(*terms):
    total = terms[0].astype(F32)
    for term in terms[1:]:
        total = total + term.astype(F32)
    return total


def reduce_by_parity(keep, send, frames):
    half = frames // 2
    keep = keep.reshape(2, half, -1, keep.shape[-1])
    got = swap_clips(send).reshape(keep.shape)
    other = summed(keep[1], got[1]).astype(BF16)
    near = lax.ppermute(other, "frame", [(i, i ^ 1) for i in range(frames)])
    mine = summed(keep[0], got[0], near).astype(BF16)
    groups = [list(range(parity, frames, 2)) for parity in range(2)]
    terms = lax.all_to_all(mine, "frame", split_axis=0, concat_axis=0, tiled=True, axis_index_groups=groups)
    return jnp.sum(terms.astype(F32), axis=0).astype(BF16)


def side_by_side(stacked, count):
    share = stacked.shape[0] // count
    return jnp.concatenate([stacked[i * share : (i + 1) * share] for i in range(count)], axis=1)


def exchange(rows, frames):
    blocks = rows.reshape(frames, -1, rows.shape[-1])
    return lax.all_to_all(blocks, "frame", split_axis=0, concat_axis=0, tiled=True)


def body(
    activations,
    cotangent,
    norm_gains,
    time_input,
    time_output,
    space_input,
    space_output,
    hidden_up,
    hidden_down,
):
    frames = lax.axis_size("frame")
    tokens, width = activations.shape[2], activations.shape[3]
    share = tokens // frames
    packed = share % 16 == 0
    tokens_all = tokens * frames * lax.axis_size("clip")
    factor = tokens_all ** (-0.5)
    groups = Groups(frames, share)
    core = jnp.stack([lax.axis_index("clip"), lax.axis_index("frame") % 2]).astype(jnp.int32)
    rows_bf = ((tokens, width), BF16)
    wide_bf = ((tokens, time_input.shape[1]), BF16)
    gain_f32 = ((1, width), F32)
    if packed:
        attention_terms = [((2 * width, width), BF16)] * 2
        mlp_terms = [((hidden_down.shape[0], width), BF16)] * 2
    else:
        attention_terms = [(time_input.shape, BF16), (time_output.shape, BF16)]
        mlp_terms = [(hidden_up.shape, BF16), (hidden_down.shape, BF16)]

    def halves(keep, send, by_parity):
        if packed:
            return (x.reshape(frames, -1, width) for x in (keep, send))
        return natural_halves(core, frames, by_parity, keep, send)

    cot = cotangent.reshape(tokens, width)
    patch_rows = exchange(activations.reshape(tokens, width), frames).reshape(tokens, width)
    first_patch, time_hidden, time_packed, time_mixed = call(
        functools.partial(time_forward_kernel, groups),
        [rows_bf, rows_bf, wide_bf, rows_bf],
        [patch_rows, norm_gains, time_input, time_output],
        flops=10**9,
        name="time_forward",
    )
    first_out = exchange(first_patch, frames).reshape(tokens, width)
    second_grad, space_hidden, space_packed, space_mixed, third_gain, mlp_keep, mlp_send = call(
        functools.partial(space_mlp_kernel, frames, factor, packed),
        [rows_bf, rows_bf, wide_bf, rows_bf, gain_f32] + mlp_terms,
        [core, first_out, cot, norm_gains, space_input, space_output, hidden_up, hidden_down],
        scalars=1,
        flops=4 * 10**9,
        name="space_mlp",
    )
    mlp_keep, mlp_send = halves(mlp_keep, mlp_send, True)
    first_grad, space_packed_grad, second_gain = call(
        space_back_kernel,
        [rows_bf, wide_bf, gain_f32],
        [first_out, second_grad, space_packed, norm_gains, space_input, space_output],
        flops=3 * 10**9,
        name="space_back",
    )
    patch_grad = exchange(first_grad, frames).reshape(tokens, width)
    space_keep, space_send = call(
        functools.partial(space_weights_kernel, frames, factor, packed),
        attention_terms,
        [core, space_hidden, space_packed_grad, space_mixed, second_grad],
        scalars=1,
        flops=10**9,
        name="space_weights",
    )
    space_keep, space_send = halves(space_keep, space_send, True)
    time_packed_grad, time_keep, time_send = call(
        functools.partial(time_back_kernel, groups, factor, packed),
        [wide_bf] + attention_terms,
        [core, patch_grad, time_hidden, time_packed, time_mixed, time_output],
        scalars=1,
        scratch=[pltpu.VMEM((tokens, width), BF16)],
        flops=2 * 10**9,
        name="time_back",
    )
    time_keep, time_send = halves(time_keep, time_send, False)
    input_patch, first_gain = call(
        time_input_kernel,
        [rows_bf, gain_f32],
        [patch_rows, patch_grad, time_packed_grad, norm_gains, time_input],
        flops=10**9,
        name="time_input",
    )

    mlp_own = reduce_by_parity(mlp_keep, mlp_send, frames)
    space_own = reduce_by_parity(space_keep, space_send, frames)

    gains = jnp.concatenate([first_gain, second_gain, third_gain], axis=0) * factor
    gains_high = gains.astype(BF16)
    gains_low = (gains - gains_high.astype(F32)).astype(BF16)
    gain_rows = jnp.concatenate([gains_high, gains_low, jnp.zeros((10, width), BF16)], axis=0)
    time_terms = summed(time_keep, swap_clips(time_send)).astype(BF16)
    last = jnp.concatenate(
        [
            time_terms,
            input_patch.reshape(frames, share, width),
            jnp.broadcast_to(gain_rows[None], (frames,) + gain_rows.shape),
        ],
        axis=1,
    )
    last = lax.all_to_all(last, "frame", split_axis=0, concat_axis=0, tiled=True)
    input_grad = last[:, 2 * share : 3 * share].reshape(activations.shape)
    time_own = jnp.sum(last[:, : 2 * share].astype(F32), axis=0).astype(BF16)
    gains_sum = jnp.sum(last[:, 3 * share :].astype(F32), axis=0)
    gains_sum = gains_sum[:3] + gains_sum[3:6]
    sum_high = gains_sum.astype(BF16)
    sum_low = (gains_sum - sum_high.astype(F32)).astype(BF16)

    own = jnp.concatenate([mlp_own, space_own], axis=0)
    got = swap_clips(own)
    tail_own = jnp.concatenate([time_own, sum_high, sum_low], axis=0)
    tail_got = swap_clips(tail_own)
    mlp_rows = mlp_own.shape[0]

    def both(mine, theirs):
        lead = core[0] == 0
        return jnp.where(lead, mine, theirs).astype(F32), jnp.where(lead, theirs, mine).astype(F32)

    up_rows, down_rows = both(own[:mlp_rows], got[:mlp_rows])
    up_grad = side_by_side(up_rows, hidden_up.shape[1] // width)

    def attention_out(mine, theirs):
        lower, upper = both(mine, theirs)
        in_grad = jnp.concatenate([lower[:share], lower[share:], upper[:share]], axis=1)
        return in_grad, upper[share:]

    space_in_grad, space_out_grad = attention_out(own[mlp_rows:], got[mlp_rows:])
    time_in_grad, time_out_grad = attention_out(tail_own[: 2 * share], tail_got[: 2 * share])
    gains_own, gains_got = tail_own[2 * share :].astype(F32), tail_got[2 * share :].astype(F32)
    gains_grad = (gains_own[:3] + gains_own[3:]) + (gains_got[:3] + gains_got[3:])
    return (
        input_grad,
        time_in_grad,
        time_out_grad,
        space_in_grad,
        space_out_grad,
        up_grad,
        down_rows,
        gains_grad,
    )


def solution(mesh):
    tokens = P(("parts", "clip"), "frame", None, None)
    owned = P(("parts", "frame"), None)
    in_specs = (tokens, tokens) + (P(),) * 7
    out_specs = (tokens,) + (owned,) * 6 + (P("parts", None),)
    return jax.shard_map(body, mesh=mesh, in_specs=in_specs, out_specs=out_specs, check_vma=False)
```

time: 590 us -> 150 us (0.25)
  waiting for transfers between devices: 350 us -> 49.8 us
  blocking collectives: 99.2 us -> 17.6 us
  matrix products: 77.5 us -> 0 us
  Pallas kernels: 0 us -> 26.4 us
  starting transfers between devices: 4.16 us -> 23.2 us
  between operations: 14.6 us -> 0.86 us
  local copies, waits for them, and re-layouts: 21.7 us -> 15 us
  other arithmetic: 21.5 us -> 15.4 us
    reduce_scatter x6 -> x0, waiting for transfers between devices: 343 us -> none  [reduce_pairs(): lax.psum_scatter(grad_term(jnp.int32(0), lax.axis_size('frame') * row_sha...]
    dot_general x27 -> x0, matrix products: 69.6 us -> none  [the longest x10 38 us: contract(): jnp.einsum(form, left_op, right_op, preferred_element_type=jnp.float32)]
    all_to_all x3 -> x1, blocking collectives: 68.4 us -> 17.6 us  [exchange(): lax.all_to_all(blocks, 'frame', split_axis=0, concat_axis=0, tiled=True)]
    all_to_all x1 -> x5, waiting for transfers between devices: 6.98 us -> 42.9 us  [the longest x1 21.9 us: body(): lax.all_to_all(last, 'frame', split_axis=0, concat_axis=0, tiled=True)]
    psum x1 -> x0, blocking collectives: 30.9 us -> none  [body(): lax.psum(jnp.stack([first_gain, second_gain, third_gain]) * factor, ('fra...]
    pallas_call x0 -> x6, Pallas kernels: none -> 26.4 us  [call(): pl.pallas_call(kernel, out_shape=[jax.ShapeDtypeStruct(shape, dtype) for...]
    all_to_all x1 -> x5, starting transfers between devices: 3.42 us -> 20.3 us  [the longest x2 9.59 us: reduce_by_parity(): lax.all_to_all(mine, 'frame', split_axis=0, concat_axis=0, tiled=True, ax...]
    another operation x8 -> x0, local copies, waits for them, and re-layouts: 10.6 us -> none  [the longest x1 3.3 us: body(): packed_patch_grad[:, None]]
  transfers between devices with their start and end apart: 9 -> 12, of which waited for: 7 -> 4; matrix products, arithmetic and copies ran while one was open for 9% -> 10% of each run, Pallas kernels for 0% -> 10%
where the time goes in v1:
time: 150 us; the launch traced here: 148 us
  waiting for transfers between devices  49.8 us (33%)
  Pallas kernels  26.4 us (18%)
  starting transfers between devices  23.2 us (15%)
  blocking collectives  17.6 us (12%)
  other arithmetic  15.4 us (10%)
  local copies, waits for them, and re-layouts  15 us (10%)
    pallas_call x6, Pallas kernels, call(): pl.pallas_call(kernel, out_shape=[jax.ShapeDtypeStruct(shape, dtype) for...  26.4 us
    all_to_all x1, waiting for transfers between devices, body(): lax.all_to_all(last, 'frame', split_axis=0, concat_axis=0, tiled=True)  21.9 us
    all_to_all x1, blocking collectives, exchange(): lax.all_to_all(blocks, 'frame', split_axis=0, concat_axis=0, tiled=True)  17.6 us
    all_to_all x2, waiting for transfers between devices, reduce_by_parity(): lax.all_to_all(mine, 'frame', split_axis=0, concat_axis=0, tiled=True, ax...  12.1 us
    unnamed x42, local copies, waits for them, and re-layouts  11.8 us
    all_to_all x2, starting transfers between devices, reduce_by_parity(): lax.all_to_all(mine, 'frame', split_axis=0, concat_axis=0, tiled=True, ax...  9.59 us
    all_to_all x2, waiting for transfers between devices, exchange(): lax.all_to_all(blocks, 'frame', split_axis=0, concat_axis=0, tiled=True)  8.84 us
    ppermute x2, waiting for transfers between devices, reduce_by_parity(): near = lax.ppermute(other, 'frame', [(i, i ^ 1) for i in range(frames)])  6.98 us
  transfers between devices with their start and end apart: 12, of which 4 were waited for; matrix products, arithmetic and copies ran while one was open for 10% of the time, Pallas kernels for 10%

profile of v1, /device:TPU:0, one launch (start us, length us, event | category | flops | bytes accessed | tf_op | source)
XLA Modules:
  0.0 148.3 jit_solution(2110307216624966362)
XLA Ops:
  0.6 17.6 %all_to_all.30 = bf16[8,48,384]{2,1,0:T(8,128)(2,1)S(1)} all-to-all(bf16[8,48,384]{2,1,0:T(8,128)(2,1)} %bitcast.39), channel_id=1, replica_groups=mesh['parts'=2,'frame'=8,'clip'=2] {'frame'}, dimensions={0} | all-to-all | bytes 589824 | tf_op jit(solution)/shard_map/all_to_all | solution.py:359
  18.3 1.2 copy-done.4
  19.4 1.0 copy-done.8
  21.1 2.8 %time_forward.1 = (bf16[384,384]{1,0:T(8,128)(2,1)}, bf16[384,384]{1,0:T(8,128)(2,1)S(1)}, bf16[384,1152]{1,0:T(8,128)(2,1)S(1)}, bf16[384,384]{1,0:T(8,128)(2,1)S(1)}) custom-call(bf16[384,384]{1,0:T(8,128)(2,1)S(1)} %bitcast.25, f32[3,384]{1,0:T(4,128)S(1)} %copy-done.10, bf16[384,1152]{1,0:T(8,128)(2,1)S(1)} %copy-done.4, bf16[384,384]{1,0:T(8,128)(2,1)S(1)} %copy-done.8), custom_call_target="tpu_custom_call" | custom-call | flops 1000000000 | bytes 4000000 | tf_op jit(solution)/shard_map/time_forward/pallas_call | solution.py:294
  26.2 3.4 %all-to-all-start.1 = ((bf16[8,48,384]{2,1,0:T(8,128)(2,1)}), bf16[8,48,384]{2,1,0:T(8,128)(2,1)S(1)}, u32[]{:S(2)}, u32[]{:S(2)}) async-start(bf16[8,48,384]{2,1,0:T(8,128)(2,1)} %bitcast.4), calls=%async_computation.1 | async-start | bytes 589824 | tf_op jit(solution)/shard_map/all_to_all | solution.py:359
  29.8 8.8 %all-to-all-done.1 = bf16[8,48,384]{2,1,0:T(8,128)(2,1)S(1)} async-done(((bf16[8,48,384]{2,1,0:T(8,128)(2,1)}), bf16[8,48,384]{2,1,0:T(8,128)(2,1)S(1)}, u32[]{:S(2)}, u32[]{:S(2)}) %all-to-all-start.1) | async-done | bytes 294944 | tf_op jit(solution)/shard_map/all_to_all | solution.py:359
  38.6 1.3 copy-done.1
  39.9 1.2 copy-done.2
  41.1 9.5 %space_mlp.1 = (bf16[384,384]{1,0:T(8,128)(2,1)S(1)}, bf16[384,384]{1,0:T(8,128)(2,1)S(1)}, bf16[384,1152]{1,0:T(8,128)(2,1)S(1)}, bf16[384,384]{1,0:T(8,128)(2,...) custom-call(s32[2]{0:T(128)S(1)} %pad_add_fusion.core_ref, ...), custom_call_target="tpu_custom_call" | custom-call | flops 4000000000 | bytes 4000000 | tf_op jit(solution)/shard_map/space_mlp/pallas_call | solution.py:294
  50.5 5.3 %space_back.1 = (bf16[384,384]{1,0:T(8,128)(2,1)}, bf16[384,1152]{1,0:T(8,128)(2,1)S(1)}, f32[1,384]{1,0:T(1,128)S(1)}) custom-call(bf16[384,384]{1,0:T(8,128)(2,1)S(1)} %bitcast.30, bf16[384,384]{1,0:T(8,128)(2,1)S(1)} %get-tuple-element.30.second_ref, bf16[384,1152]{1,0:T(8,128)(2,1)S(1)} %get-tuple-element.31.packed_ref, f32[3,384]{1,0:T(4,128)S(1)} %copy-done.11, ...), custom_call_target="tpu_custom_call" | custom-call | flops 3000000000 | bytes 4000000 | tf_op jit(solution)/shard_map/space_back/pallas_call | solution.py:294
  55.8 1.6 %space_weights.1 = (bf16[768,384]{1,0:T(8,128)(2,1)S(1)}, bf16[768,384]{1,0:T(8,128)(2,1)S(1)}) custom-call(s32[2]{0:T(128)S(1)} %pad_add_fusion.core_ref, bf16[384,384]{1,0:T(8,128)(2,1)S(1)} %get-tuple-element.43.hidden_ref, bf16[384,1152]{1,0:T(8,128)(2,1)S(1)} %get-tuple-element.44.packed_grad_ref, bf16[384,384]{1,0:T(8,128)(2,1)S(1)} %get-tuple-element.45.mixed_ref, ...), custom_call_target="tpu_custom_call" | custom-call | flops 1000000000 | bytes 4000000 | tf_op jit(solution)/shard_map/space_weights/pallas_call | solution.py:294
  58.0 3.5 %all-to-all-start.2 = ((bf16[8,48,384]{2,1,0:T(8,128)(2,1)}), bf16[8,48,384]{2,1,0:T(8,128)(2,1)S(1)}, u32[]{:S(2)}, u32[]{:S(2)}) async-start(bf16[8,48,384]{2,1,0:T(8,128)(2,1)} %bitcast.7), calls=%async_computation.2 | async-start | bytes 589824 | tf_op jit(solution)/shard_map/all_to_all | solution.py:359
  61.6 0.9 fusion.11
  62.6 1.0 fusion.4
  63.6 2.1 %collective-permute-start.3 = (bf16[4,96,384]{2,1,0:T(8,128)(2,1)S(1)}, bf16[4,96,384]{2,1,0:T(8,128)(2,1)S(1)}, u32[]{:S(2)}, u32[]{:S(2)}) collective-permute-start(bf16[4,96,384]{2,1,0:T(8,128)(2,1)S(1)} %fusion.4), channel_id=1, source_target_pairs={{0,2},{2,0},{4,6},{6,4},{8,10},{10,8},{12,14},{14,12},{1,3},{3,1},... | collective-permute-start | bytes 884744 | tf_op jit(solution)/shard_map/ppermute | solution.py:345
  65.7 2.0 %fusion = bf16[4,192,384]{2,1,0:T(8,128)(2,1)} fusion(bf16[4,192,384]{2,1,0:T(8,128)(2,1)S(1)} %bitcast.35, bf16[8,192,384]{2,1,0:T(8,128)(2,1)} %collective-permute-done.4), kind=kLoop, calls=%fused_computation.1 | loop fusion | flops 1179648 | bytes 1769472 | tf_op jit(solution)/shard_map/convert_element_type | solution.py:344
  67.8 7.0 %collective-permute-done.3 = bf16[4,96,384]{2,1,0:T(8,128)(2,1)S(1)} collective-permute-done((bf16[4,96,384]{2,1,0:T(8,128)(2,1)S(1)}, bf16[4,96,384]{2,1,0:T(8,128)(2,1)S(1)}, u32[]{:S(2)}, u32[]{:S(2)}) %collective-permute-start.3) | collective-permute-done | bytes 294944 | tf_op jit(solution)/shard_map/ppermute | solution.py:345
  74.7 1.8 %fusion.6 = bf16[4,96,384]{2,1,0:T(8,128)(2,1)} fusion(bf16[4,96,384]{2,1,0:T(8,128)(2,1)S(1)} %bitcast.38, bf16[4,96,384]{2,1,0:T(8,128)(2,1)S(1)} %collective-permute-done.3, bf16[8,96,384]{2,1,0:T(8,128)(2,1)} %collective-permute-done.2), kind=kLoop, calls=%fused_computation.13 | loop fusion | flops 884736 | bytes 1179648 | tf_op jit(solution)/shard_map/convert_element_type | solution.py:346
  76.5 4.4 %all-to-all-start.4 = ((bf16[4,96,384]{2,1,0:T(8,128)(2,1)}), bf16[4,96,384]{2,1,0:T(8,128)(2,1)}, u32[]{:S(2)}, u32[]{:S(2)}) async-start(bf16[4,96,384]{2,1,0:T(8,128)(2,1)} %fusion.6), calls=%async_computation.4 | async-start | bytes 589824 | tf_op jit(solution)/shard_map/all_to_all | solution.py:348
  80.9 1.2 copy-done.15
  82.1 1.0 copy-done.19
  83.0 6.3 %time_back.1 = (bf16[384,1152]{1,0:T(8,128)(2,1)S(1)}, bf16[768,384]{1,0:T(8,128)(2,1)S(1)}, bf16[768,384]{1,0:T(8,128)(2,1)S(1)}) custom-call(s32[2]{0:T(128)S(1)} %pad_add_fusion.core_ref, bf16[384,384]{1,0:T(8,128)(2,1)S(1)} %bitcast.27, bf16[384,384]{1,0:T(8,128)(2,1)S(1)} %copy-done.17, bf16[384,1152]{1,0:T(8,128)(2,1)S(1)} %copy-done.15, ...), custom_call_target="tpu_custom_call" | custom-call | flops 2000000000 | bytes 4000000 | tf_op jit(solution)/shard_map/time_back/pallas_call | solution.py:294
  90.3 2.3 %fusion.2 = bf16[4,192,384]{2,1,0:T(8,128)(2,1)} fusion(bf16[4,192,384]{2,1,0:T(8,128)(2,1)S(1)} %bitcast.36, bf16[4,192,384]{2,1,0:T(8,128)(2,1)} %collective-permute-done.5, bf16[8,192,384]{2,1,0:T(8,128)(2,1)} %collective-permute-done.4), kind=kLoop, calls=%fused_computation.4 | loop fusion | flops 1769472 | bytes 2359296 | tf_op jit(solution)/shard_map/convert_element_type | solution.py:346
  92.6 5.2 %all-to-all-start.5 = ((bf16[4,192,384]{2,1,0:T(8,128)(2,1)}), bf16[4,192,384]{2,1,0:T(8,128)(2,1)}, u32[]{:S(2)}, u32[]{:S(2)}) async-start(bf16[4,192,384]{2,1,0:T(8,128)(2,1)} %fusion.2), calls=%async_computation.5 | async-start | bytes 1179648 | tf_op jit(solution)/shard_map/all_to_all | solution.py:348
  97.9 1.2 copy-done.13
  100.0 1.2 fusion.3
  101.3 1.1 pad_maximum_fusion
  102.3 12.1 %all-to-all-done.5 = bf16[4,192,384]{2,1,0:T(8,128)(2,1)} async-done(((bf16[4,192,384]{2,1,0:T(8,128)(2,1)}), bf16[4,192,384]{2,1,0:T(8,128)(2,1)}, u32[]{:S(2)}, u32[]{:S(2)}) %all-to-all-start.5) | async-done | bytes 589856 | tf_op jit(solution)/shard_map/all_to_all | solution.py:348
  114.5 3.8 %all-to-all-start.3 = ((bf16[8,160,384]{2,1,0:T(8,128)(2,1)}), bf16[8,160,384]{2,1,0:T(8,128)(2,1)S(1)}, u32[]{:S(2)}, u32[]{:S(2)}) async-start(bf16[8,160,384]{2,1,0:T(8,128)(2,1)} %pad_maximum_fusion), calls=%async_computation.3 | async-start | bytes 1966080 | tf_op jit(solution)/shard_map/all_to_all | solution.py:466
  118.2 1.0 reduce_sum.47
  119.3 1.2 reduce_sum.48
  120.5 21.9 %all-to-all-done.3 = bf16[8,160,384]{2,1,0:T(8,128)(2,1)S(1)} async-done(((bf16[8,160,384]{2,1,0:T(8,128)(2,1)}), bf16[8,160,384]{2,1,0:T(8,128)(2,1)S(1)}, u32[]{:S(2)}, u32[]{:S(2)}) %all-to-all-start.3) | async-done | bytes 983072 | tf_op jit(solution)/shard_map/all_to_all | solution.py:466
  (76 shorter events, 11.7 us)
Async XLA Ops:
  18.3 1.2 copy-start.4
  19.4 1.0 copy-start.8
  21.1 17.5 %copy-start = (bf16[384,1536]{1,0:T(8,128)(2,1)S(1)}, bf16[384,1536]{1,0:T(8,128)(2,1)}, u32[]{:S(2)}) copy-start(bf16[384,1536]{1,0:T(8,128)(2,1)} %up_ref.1) | copy-start | bytes 3538948
  21.1 17.5 %copy-start.6 = (bf16[1,1,384,384]{3,2,1,0:T(8,128)(2,1)S(1)}, bf16[1,1,384,384]{3,2,1,0:T(8,128)(2,1)}, u32[]{:S(2)}) copy-start(bf16[1,1,384,384]{3,2,1,0:T(8,128)(2,1)} %param.10) | copy-start | bytes 884740
  21.1 17.5 %copy-start.7 = (bf16[384,384]{1,0:T(8,128)(2,1)S(1)}, bf16[384,384]{1,0:T(8,128)(2,1)}, u32[]{:S(2)}) copy-start(bf16[384,384]{1,0:T(8,128)(2,1)} %out_ref.6) | copy-start | bytes 884740
  21.1 17.5 %copy-start.11 = (f32[3,384]{1,0:T(4,128)S(1)}, f32[3,384]{1,0:T(4,128)}, u32[]{:S(2)}) copy-start(f32[3,384]{1,0:T(4,128)} %gains_ref.7) | copy-start | bytes 13828
  23.9 0.9 copy-start.14
  24.8 0.7 copy-start.16
  25.5 0.7 copy-start.18
  26.2 12.4 %all-to-all-start.1 = ((bf16[8,48,384]{2,1,0:T(8,128)(2,1)}), bf16[8,48,384]{2,1,0:T(8,128)(2,1)S(1)}, u32[]{:S(2)}, u32[]{:S(2)}) async-start(bf16[8,48,384]{2,1,0:T(8,128)(2,1)} %bitcast.4), calls=%async_computation.1 | async-start | bytes 589824 | tf_op jit(solution)/shard_map/all_to_all | solution.py:359
  38.6 1.3 copy-start.1
  39.9 1.2 copy-start.2
  41.1 9.5 %copy-start.3 = (bf16[384,1152]{1,0:T(8,128)(2,1)S(1)}, bf16[384,1152]{1,0:T(8,128)(2,1)}, u32[]{:S(2)}) copy-start(bf16[384,1152]{1,0:T(8,128)(2,1)} %in_ref.6) | copy-start | bytes 2654212
  50.5 15.2 %collective-permute-start.4 = (bf16[8,192,384]{2,1,0:T(8,128)(2,1)}, bf16[8,192,384]{2,1,0:T(8,128)(2,1)}, u32[]{:S(2)}, u32[]{:S(2)}) collective-permute-start(bf16[8,192,384]{2,1,0:T(8,128)(2,1)} %bitcast.17), channel_id=1, source_target_pairs={{0,1},{1,0},{2,3},{3,2},{4,5},{5,4},{6,7},{7,6},{8,9},{9,8},{10,11... | collective-permute-start | bytes 3538952 | tf_op jit(solution)/shard_map/ppermute | solution.py:330
  57.5 5.1 %collective-permute-start.2 = (bf16[8,96,384]{2,1,0:T(8,128)(2,1)S(1)}, bf16[8,96,384]{2,1,0:T(8,128)(2,1)}, u32[]{:S(2)}, u32[]{:S(2)}) collective-permute-start(bf16[8,96,384]{2,1,0:T(8,128)(2,1)S(1)} %bitcast.33), channel_id=1, source_target_pairs={{0,1},{1,0},{2,3},{3,2},{4,5},{5,4},{6,7},{7,6},{8,9},{9,8},{10,11... | collective-permute-start | bytes 1769480 | tf_op jit(solution)/shard_map/ppermute | solution.py:330
  58.0 18.5 %all-to-all-start.2 = ((bf16[8,48,384]{2,1,0:T(8,128)(2,1)}), bf16[8,48,384]{2,1,0:T(8,128)(2,1)S(1)}, u32[]{:S(2)}, u32[]{:S(2)}) async-start(bf16[8,48,384]{2,1,0:T(8,128)(2,1)} %bitcast.7), calls=%async_computation.2 | async-start | bytes 589824 | tf_op jit(solution)/shard_map/all_to_all | solution.py:359
  63.6 11.1 %collective-permute-start.3 = (bf16[4,96,384]{2,1,0:T(8,128)(2,1)S(1)}, bf16[4,96,384]{2,1,0:T(8,128)(2,1)S(1)}, u32[]{:S(2)}, u32[]{:S(2)}) collective-permute-start(bf16[4,96,384]{2,1,0:T(8,128)(2,1)S(1)} %fusion.4), channel_id=1, source_target_pairs={{0,2},{2,0},{4,6},{6,4},{8,10},{10,8},{12,14},{14,12},{1,3},{3,1},... | collective-permute-start | bytes 884744 | tf_op jit(solution)/shard_map/ppermute | solution.py:345
  67.7 13.2 %copy-start.9 = (bf16[384,384]{1,0:T(8,128)(2,1)S(1)}, bf16[384,384]{1,0:T(8,128)(2,1)}, u32[]{:S(2)}) copy-start(bf16[384,384]{1,0:T(8,128)(2,1)} %out_ref.7) | copy-start | bytes 884740
  67.7 13.2 %copy-start.17 = (bf16[384,384]{1,0:T(8,128)(2,1)S(1)}, bf16[384,384]{1,0:T(8,128)(2,1)}, u32[]{:S(2)}) copy-start(bf16[384,384]{1,0:T(8,128)(2,1)} %copy-done.16) | copy-start | bytes 884740
  67.7 22.5 %collective-permute-start.5 = (bf16[4,192,384]{2,1,0:T(8,128)(2,1)}, bf16[4,192,384]{2,1,0:T(8,128)(2,1)}, u32[]{:S(2)}, u32[]{:S(2)}) collective-permute-start(bf16[4,192,384]{2,1,0:T(8,128)(2,1)} %fusion), channel_id=1, source_target_pairs={{0,2},{2,0},{4,6},{6,4},{8,10},{10,8},{12,14},{14,12},{1,3},{3,1},... | collective-permute-start | bytes 1769480 | tf_op jit(solution)/shard_map/ppermute | solution.py:345
  76.5 16.0 %all-to-all-start.4 = ((bf16[4,96,384]{2,1,0:T(8,128)(2,1)}), bf16[4,96,384]{2,1,0:T(8,128)(2,1)}, u32[]{:S(2)}, u32[]{:S(2)}) async-start(bf16[4,96,384]{2,1,0:T(8,128)(2,1)} %fusion.6), calls=%async_computation.4 | async-start | bytes 589824 | tf_op jit(solution)/shard_map/all_to_all | solution.py:348
  80.9 1.2 copy-start.15
  82.1 1.0 copy-start.19
  83.0 7.2 %copy-start.20 = (bf16[768,384]{1,0:T(8,128)(2,1)S(1)}, bf16[768,384]{1,0:T(8,128)(2,1)}, u32[]{:S(2)}) copy-start(bf16[768,384]{1,0:T(8,128)(2,1)} %get-tuple-element.53) | copy-start | bytes 1769476
  89.3 0.9 copy-start.12
  90.3 9.8 %collective-permute-start = (bf16[8,96,384]{2,1,0:T(8,128)(2,1)S(1)}, bf16[8,96,384]{2,1,0:T(8,128)(2,1)}, u32[]{:S(2)}, u32[]{:S(2)}) collective-permute-start(bf16[8,96,384]{2,1,0:T(8,128)(2,1)S(1)} %bitcast.32), channel_id=1, source_target_pairs={{0,1},{1,0},{2,3},{3,2},{4,5},{5,4},{6,7},{7,6},{8,9},{9,8},{10,11... | collective-permute-start | bytes 1769480 | tf_op jit(solution)/shard_map/ppermute | solution.py:330
  92.6 5.3 %copy-start.5 = (bf16[384,1152]{1,0:T(8,128)(2,1)S(1)}, bf16[384,1152]{1,0:T(8,128)(2,1)}, u32[]{:S(2)}) copy-start(bf16[384,1152]{1,0:T(8,128)(2,1)} %in_ref.7) | copy-start | bytes 2654212
  92.6 21.9 %all-to-all-start.5 = ((bf16[4,192,384]{2,1,0:T(8,128)(2,1)}), bf16[4,192,384]{2,1,0:T(8,128)(2,1)}, u32[]{:S(2)}, u32[]{:S(2)}) async-start(bf16[4,192,384]{2,1,0:T(8,128)(2,1)} %fusion.2), calls=%async_computation.5 | async-start | bytes 1179648 | tf_op jit(solution)/shard_map/all_to_all | solution.py:348
  97.9 1.2 copy-start.13
  114.5 27.9 %all-to-all-start.3 = ((bf16[8,160,384]{2,1,0:T(8,128)(2,1)}), bf16[8,160,384]{2,1,0:T(8,128)(2,1)S(1)}, u32[]{:S(2)}, u32[]{:S(2)}) async-start(bf16[8,160,384]{2,1,0:T(8,128)(2,1)} %pad_maximum_fusion), calls=%async_computation.3 | async-start | bytes 1966080 | tf_op jit(solution)/shard_map/all_to_all | solution.py:466
  120.4 22.9 %collective-permute-start.6 = (bf16[288,384]{1,0:T(8,128)(2,1)S(1)}, bf16[288,384]{1,0:T(8,128)(2,1)S(1)}, u32[]{:S(2)}, u32[]{:S(2)}) collective-permute-start(bf16[288,384]{1,0:T(8,128)(2,1)S(1)} %pad_maximum_fusion.3), channel_id=1, source_target_pairs={{0,1},{1,0},{2,3},{3,2},{4,5},{5,4},{6,7},{7,6},{8,9},{9,8},{10,11... | collective-permute-start | bytes 663560 | tf_op jit(solution)/shard_map/ppermute | solution.py:330
  142.5 2.4 %collective-permute-start.1 = (bf16[102,384]{1,0:T(8,128)(2,1)S(1)}, bf16[102,384]{1,0:T(8,128)(2,1)S(1)}, u32[]{:S(2)}, u32[]{:S(2)}) collective-permute-start(bf16[102,384]{1,0:T(8,128)(2,1)S(1)} %pad_maximum_fusion.5), channel_id=1, source_target_pairs={{0,1},{1,0},{2,3},{3,2},{4,5},{5,4},{6,7},{7,6},{8,9},{9,8},{10,11... | collective-permute-start | bytes 235016 | tf_op jit(solution)/shard_map/ppermute | solution.py:330
  (1 other events, 0.7 us)

commit v2 on v1

v2 whole, which is shorter than its diff:
```python
import functools

import jax
import jax.numpy as jnp
from jax import lax
from jax.experimental import pallas as pl
from jax.experimental.pallas import tpu as pltpu
from jax.sharding import PartitionSpec as P

HEADS = 6
HEAD_DIM = 64
SCALE = HEAD_DIM ** (-0.5)
EPSILON = 1e-06
GELU_C = 0.7978845608028654
GELU_A = 0.044715
MASKED = -1e30
F32 = jnp.float32
BF16 = jnp.bfloat16


def nn(a, b):
    return lax.dot_general(a, b, (((1,), (0,)), ((), ())), preferred_element_type=F32)


def nt(a, b):
    return lax.dot_general(a, b, (((1,), (1,)), ((), ())), preferred_element_type=F32)


def tn(a, b):
    return lax.dot_general(a, b, (((0,), (0,)), ((), ())), preferred_element_type=F32)


def normalize(rows):
    offset = rows - jnp.mean(rows, axis=-1, keepdims=True)
    inverse = lax.rsqrt(jnp.mean(offset * offset, axis=-1, keepdims=True) + EPSILON)
    return offset * inverse, inverse


def normalize_back(hidden_grad, normed, inverse, gain):
    scaled = hidden_grad * gain
    return inverse * (
        scaled
        - jnp.mean(scaled, axis=-1, keepdims=True)
        - normed * jnp.mean(scaled * normed, axis=-1, keepdims=True)
    )


def lane_masks(dtype):
    lane = lax.broadcasted_iota(jnp.int32, (1, 2 * HEAD_DIM), 1)
    first = (lane < HEAD_DIM).astype(F32)
    return first.astype(dtype), (1.0 - first).astype(dtype)


def both_heads(pair):
    first, second = lane_masks(pair.dtype)
    return jnp.concatenate([pair * first, pair * second], axis=0)


def merge_heads(stacked):
    first, second = lane_masks(stacked.dtype)
    count = stacked.shape[0] // 2
    return stacked[:count] * first + stacked[count:] * second


def pair_attend(queries, keys, values, mask):
    scores = nt(both_heads(keys), queries * jnp.asarray(SCALE, BF16))
    count = keys.shape[0]
    shares = []
    for half in (scores[:count], scores[count:]):
        if mask is not None:
            half = jnp.where(mask, half, MASKED)
        raised = jnp.exp(half - jnp.max(half, axis=0, keepdims=True))
        shares.append((raised * (1.0 / jnp.sum(raised, axis=0, keepdims=True))).astype(BF16))
    shares = jnp.concatenate(shares, axis=0)
    return tn(shares, both_heads(values)).astype(BF16), shares


def pair_attend_back(queries, keys, values, mixed_grad, shares):
    count = keys.shape[0]
    share_grad = nt(both_heads(values), mixed_grad)
    score_grads = []
    for start in (0, count):
        share = shares[start : start + count].astype(F32)
        grad = share_grad[start : start + count]
        row = jnp.sum(grad * share, axis=0, keepdims=True)
        score_grads.append((share * (grad - row) * SCALE).astype(BF16))
    score_grad = jnp.concatenate(score_grads, axis=0)
    query_grad = tn(score_grad, both_heads(keys))
    key_grad = merge_heads(nn(score_grad, queries))
    value_grad = merge_heads(nn(shares, mixed_grad))
    return query_grad.astype(BF16), key_grad.astype(BF16), value_grad.astype(BF16)


class Groups:
    def __init__(self, frames, share):
        self.frames, self.share = frames, share
        self.size = 16 if share % 16 == 0 else share
        self.count = share // self.size

    def mask(self):
        rows = self.frames * self.size
        i = lax.broadcasted_iota(jnp.int32, (rows, rows), 0)
        j = lax.broadcasted_iota(jnp.int32, (rows, rows), 1)
        return lax.rem(i, self.size) == lax.rem(j, self.size)

    def load(self, ref, group, first, width):
        parts = [
            ref[pl.ds(f * self.share + group * self.size, self.size), pl.ds(first, width)]
            for f in range(self.frames)
        ]
        if self.count == 1:
            return ref[:, pl.ds(first, width)]
        return jnp.concatenate(parts, axis=0)

    def store(self, ref, group, first, value):
        if self.count == 1:
            ref[:, pl.ds(first, value.shape[1])] = value
            return
        for f in range(self.frames):
            ref[pl.ds(f * self.share + group * self.size, self.size), pl.ds(first, value.shape[1])] = value[
                f * self.size : (f + 1) * self.size
            ]


def active_grad_kernel(cot_ref, down_ref, grad_ref):
    grad_ref[...] = nt(cot_ref[...], down_ref[...])


def time_forward_kernel(
    groups, x_ref, gains_ref, in_ref, out_ref, first_ref, hidden_ref, packed_ref, mixed_ref, shares_ref
):
    rows = x_ref[...].astype(F32)
    width = rows.shape[1]
    normed, _ = normalize(rows)
    hidden = (normed * gains_ref[0:1, :]).astype(BF16)
    hidden_ref[...] = hidden
    packed_ref[...] = nn(hidden, in_ref[...]).astype(BF16)
    mask = groups.mask()
    block = 0
    for group in range(groups.count):
        for first in range(0, width, 2 * HEAD_DIM):
            q, k, v = (groups.load(packed_ref, group, part * width + first, 2 * HEAD_DIM) for part in range(3))
            mixed, shares = pair_attend(q, k, v, mask)
            groups.store(mixed_ref, group, first, mixed)
            shares_ref[pl.ds(block, shares.shape[0]), :] = shares
            block += shares.shape[0]
    send(hidden_ref, packed_ref, mixed_ref, shares_ref)
    first_ref[...] = (rows + nn(mixed_ref[...], out_ref[...])).astype(BF16)


def store_half(core_ref, half, keep_ref, send_ref, store):
    @pl.when(core_ref[0] == half)
    def _():
        store(keep_ref)

    @pl.when(core_ref[0] != half)
    def _():
        store(send_ref)


def fold_bits(frames):
    return list(range(frames.bit_length() - 1))


def fold_place(apart, frames):
    bits = fold_bits(frames)
    place = 0
    for index, bit in enumerate(bits):
        place = place + (((apart >> bit) & 1) << (len(bits) - 1 - index))
    return place


def block_place(core_ref, owner, frames, rows, folded):
    if not folded:
        return owner * rows
    return pl.multiple_of(fold_place(owner ^ core_ref[1], frames) * rows, rows)


def pack_columns(core_ref, frames, columns, ref, folded):
    share = columns[0].shape[0] // frames
    for owner in range(frames):
        place = block_place(core_ref, owner, frames, share * len(columns), folded)
        for index, piece in enumerate(columns):
            start = place + index * share
            if folded:
                start = pl.multiple_of(start, share)
            ref[pl.ds(start, share), :] = piece[owner * share : (owner + 1) * share]


def pack_rows(core_ref, frames, tall, ref):
    rows = tall.shape[0] // frames
    for owner in range(frames):
        start = block_place(core_ref, owner, frames, rows, True)
        ref[pl.ds(start, rows), :] = tall[owner * rows : (owner + 1) * rows]


def space_mlp_kernel(
    frames, factor, packed_grads,
    core_ref, x_ref, cot_ref, gains_ref, in_ref, out_ref, up_ref, active_grad_ref,
    grad_ref, hidden_ref, packed_ref, mixed_ref, shares_ref, gain_ref, keep_ref, send_ref,
):
    rows = x_ref[...].astype(F32)
    width = rows.shape[1]
    normed, _ = normalize(rows)
    hidden = (normed * gains_ref[1:2, :]).astype(BF16)
    hidden_ref[...] = hidden
    packed_ref[...] = nn(hidden, in_ref[...]).astype(BF16)
    for first in range(0, width, 2 * HEAD_DIM):
        q, k, v = (packed_ref[:, pl.ds(part * width + first, 2 * HEAD_DIM)] for part in range(3))
        mixed, shares = pair_attend(q, k, v, None)
        mixed_ref[:, pl.ds(first, 2 * HEAD_DIM)] = mixed
        shares_ref[pl.ds(first // (2 * HEAD_DIM) * shares.shape[0], shares.shape[0]), :] = shares
    second = (rows + nn(mixed_ref[...], out_ref[...])).astype(BF16)
    normed, inverse = normalize(second.astype(F32))
    gain = gains_ref[2:3, :]
    mlp_hidden = (normed * gain).astype(BF16)
    before = nn(mlp_hidden, up_ref[...])
    square = before * before
    bent = jnp.tanh(GELU_C * before * (1.0 + GELU_A * square))
    half_bent = 0.5 + 0.5 * bent
    active = (before * half_bent).astype(BF16)
    slope = half_bent + 0.5 * before * (1.0 - bent * bent) * (GELU_C * (1.0 + 3.0 * GELU_A * square))
    cot = cot_ref[...]
    before_grad = (slope * active_grad_ref[...]).astype(BF16)
    hidden_grad = nt(before_grad, up_ref[...])
    gain_ref[...] = jnp.sum(hidden_grad * normed, axis=0, keepdims=True)
    send(hidden_ref, mixed_ref, gain_ref)
    grad_ref[...] = (cot.astype(F32) + normalize_back(hidden_grad, normed, inverse, gain)).astype(BF16)
    up_grad = (tn(mlp_hidden, before_grad) * factor).astype(BF16)
    down_grad = (tn(active, cot) * factor).astype(BF16)
    if packed_grads:
        pieces = [up_grad[:, first : first + width] for first in range(0, up_grad.shape[1], width)]
        store_half(core_ref, 0, keep_ref, send_ref, lambda ref: pack_columns(core_ref, frames, pieces, ref, True))
        store_half(core_ref, 1, keep_ref, send_ref, lambda ref: pack_rows(core_ref, frames, down_grad, ref))
    else:
        keep_ref[...] = up_grad
        send_ref[...] = down_grad


def space_back_kernel(
    x_ref, second_ref, packed_ref, shares_ref, gains_ref, in_ref, out_ref, grad_ref, packed_grad_ref, gain_ref
):
    second = second_ref[...]
    width = second.shape[1]
    mixed_grad = nt(second, out_ref[...]).astype(BF16)
    for first in range(0, width, 2 * HEAD_DIM):
        q, k, v = (packed_ref[:, pl.ds(part * width + first, 2 * HEAD_DIM)] for part in range(3))
        start = first // (2 * HEAD_DIM) * 2 * second.shape[0]
        shares = shares_ref[pl.ds(start, 2 * second.shape[0]), :]
        grads = pair_attend_back(q, k, v, mixed_grad[:, first : first + 2 * HEAD_DIM], shares)
        for part, grad in enumerate(grads):
            packed_grad_ref[:, pl.ds(part * width + first, 2 * HEAD_DIM)] = grad
    send(packed_grad_ref)
    hidden_grad = nt(packed_grad_ref[...], in_ref[...])
    normed, inverse = normalize(x_ref[...].astype(F32))
    gain_ref[...] = jnp.sum(hidden_grad * normed, axis=0, keepdims=True)
    grad_ref[...] = (
        second.astype(F32) + normalize_back(hidden_grad, normed, inverse, gains_ref[1:2, :])
    ).astype(BF16)


def store_attention_grads(core_ref, frames, packed_grads, folded, in_grad, out_grad, keep_ref, send_ref):
    width = out_grad.shape[1]
    if packed_grads:
        pieces = [in_grad[:, first : first + width] for first in range(0, in_grad.shape[1], width)] + [out_grad]
        for half in range(2):
            store_half(
                core_ref, half, keep_ref, send_ref,
                lambda ref, half=half: pack_columns(
                    core_ref, frames, pieces[2 * half : 2 * half + 2], ref, folded
                ),
            )
    else:
        keep_ref[...] = in_grad
        send_ref[...] = out_grad


def space_weights_kernel(
    frames, factor, packed_grads, core_ref, hidden_ref, packed_grad_ref, mixed_ref, second_ref, keep_ref, send_ref
):
    in_grad = (tn(hidden_ref[...], packed_grad_ref[...]) * factor).astype(BF16)
    out_grad = (tn(mixed_ref[...], second_ref[...]) * factor).astype(BF16)
    store_attention_grads(core_ref, frames, packed_grads, True, in_grad, out_grad, keep_ref, send_ref)


def time_back_kernel(
    groups, factor, packed_grads,
    core_ref, grad_ref, hidden_ref, packed_ref, mixed_ref, shares_ref, out_ref,
    packed_grad_ref, keep_ref, send_ref, mixed_grad_ref,
):
    grad = grad_ref[...]
    width = grad.shape[1]
    mixed_grad_ref[...] = nt(grad, out_ref[...]).astype(BF16)
    rows = 2 * groups.frames * groups.size
    block = 0
    for group in range(groups.count):
        for first in range(0, width, 2 * HEAD_DIM):
            q, k, v = (groups.load(packed_ref, group, part * width + first, 2 * HEAD_DIM) for part in range(3))
            part_grad = groups.load(mixed_grad_ref, group, first, 2 * HEAD_DIM)
            grads = pair_attend_back(q, k, v, part_grad, shares_ref[pl.ds(block, rows), :])
            block += rows
            for part, value in enumerate(grads):
                groups.store(packed_grad_ref, group, part * width + first, value)
    in_grad = (tn(hidden_ref[...], packed_grad_ref[...]) * factor).astype(BF16)
    out_grad = (tn(mixed_ref[...], grad) * factor).astype(BF16)
    store_attention_grads(core_ref, groups.frames, packed_grads, False, in_grad, out_grad, keep_ref, send_ref)


def time_input_kernel(x_ref, grad_ref, packed_grad_ref, gains_ref, in_ref, input_ref, gain_ref):
    hidden_grad = nt(packed_grad_ref[...], in_ref[...])
    normed, inverse = normalize(x_ref[...].astype(F32))
    gain_ref[...] = jnp.sum(hidden_grad * normed, axis=0, keepdims=True)
    input_ref[...] = (
        grad_ref[...].astype(F32) + normalize_back(hidden_grad, normed, inverse, gains_ref[0:1, :])
    ).astype(BF16)


class Arriving:
    def __init__(self, source, target, semaphore):
        self.target, self.copy = target, pltpu.make_async_copy(source, target, semaphore)
        self.copy.start()
        self.waited = False

    def wait(self):
        if not self.waited:
            self.copy.wait()
            self.waited = True

    def __getitem__(self, index):
        self.wait()
        return self.target[index]


class Leaving:
    def __init__(self, source, target, semaphore):
        self.source, self.copy = source, pltpu.make_async_copy(source, target, semaphore)
        self.sent = False

    def send(self):
        if not self.sent:
            self.copy.start()
            self.sent = True

    def __getitem__(self, index):
        return self.source[index]

    def __setitem__(self, index, value):
        self.source[index] = value


def send(*refs):
    for ref in refs:
        if isinstance(ref, Leaving):
            ref.send()


def call(kernel, outs, args, scalars=0, scratch=(), vmem=16, name=None, far_in=(), far_out=()):
    near, far = pl.BlockSpec(memory_space=pltpu.VMEM), pl.BlockSpec(memory_space=pltpu.HBM)
    in_specs = [pl.BlockSpec(memory_space=pltpu.SMEM)] * scalars
    in_specs += [far if i in far_in else near for i in range(scalars, len(args))]
    staging = [pltpu.VMEM(args[i].shape, args[i].dtype) for i in far_in]
    staging += [pltpu.VMEM(*outs[i]) for i in far_out]
    count = len(args) + len(outs)

    def staged(*refs):
        refs, extra, stages, semaphores = (
            list(refs[:count]),
            refs[count : count + len(scratch)],
            refs[count + len(scratch) : count + len(scratch) + len(staging)],
            refs[-1],
        )
        leaving = []
        for k, i in enumerate(far_in):
            refs[i] = Arriving(refs[i], stages[k], semaphores.at[k])
        for k, i in enumerate(far_out):
            k += len(far_in)
            refs[len(args) + i] = Leaving(stages[k], refs[len(args) + i], semaphores.at[k])
            leaving.append(refs[len(args) + i])
        kernel(*refs, *extra)
        for i in far_in:
            refs[i].wait()
        for ref in leaving:
            ref.send()
        for ref in leaving:
            ref.copy.wait()

    args = [pltpu.with_memory_space_constraint(a, pltpu.HBM) if i in far_in else a for i, a in enumerate(args)]
    return pl.pallas_call(
        staged,
        out_shape=[
            pltpu.HBM(shape, dtype) if i in far_out else jax.ShapeDtypeStruct(shape, dtype)
            for i, (shape, dtype) in enumerate(outs)
        ],
        in_specs=in_specs,
        out_specs=[far if i in far_out else near for i in range(len(outs))],
        scratch_shapes=list(scratch) + staging + [pltpu.SemaphoreType.DMA((max(len(staging), 1),))],
        compiler_params=pltpu.CompilerParams(vmem_limit_bytes=vmem * 1024 * 1024),
        cost_estimate=CHEAP,
        name=name,
    )(*args)


def prefetch_kernel(count, *refs):
    sources, targets, semaphores = refs[:count], refs[count : 2 * count], refs[-1]
    copies = [pltpu.make_async_copy(sources[i], targets[i], semaphores.at[i]) for i in range(count)]
    for copy in copies:
        copy.start()
    for copy in copies:
        copy.wait()


def prefetch(*arrays):
    return pl.pallas_call(
        functools.partial(prefetch_kernel, len(arrays)),
        out_shape=[pltpu.VMEM(a.shape, a.dtype) for a in arrays],
        in_specs=[pl.BlockSpec(memory_space=pltpu.HBM)] * len(arrays),
        out_specs=[pl.BlockSpec(memory_space=pltpu.VMEM)] * len(arrays),
        scratch_shapes=[pltpu.SemaphoreType.DMA((len(arrays),))],
        compiler_params=pltpu.CompilerParams(vmem_limit_bytes=1024 * 1024),
        cost_estimate=CHEAP,
        name="prefetch",
    )(*[pltpu.with_memory_space_constraint(a, pltpu.HBM) for a in arrays])


def natural_halves(core, frames, folded, first, second):
    width = min(first.shape[1], second.shape[1])

    def blocks(matrix):
        matrix = matrix.reshape(frames, matrix.shape[0] // frames, -1, width)
        return jnp.swapaxes(matrix, 1, 2).reshape(frames, -1, width)

    first, second = blocks(first), blocks(second)
    if first.shape != second.shape:
        whole = jnp.concatenate([first, second], axis=1)
        middle = whole.shape[1] // 2
        first, second = whole[:, :middle], whole[:, middle:]
    if folded:
        places = jnp.stack([fold_place(jnp.int32(owner) ^ core[1], frames) for owner in range(frames)])
        first, second = (jnp.zeros_like(blocked).at[places].set(blocked) for blocked in (first, second))
    swap = core[0] == 0
    return jnp.where(swap, first, second), jnp.where(swap, second, first)


def swap_clips(array):
    return lax.ppermute(array, "clip", [(0, 1), (1, 0)])


CHEAP = pl.CostEstimate(flops=1000, transcendentals=0, bytes_accessed=1000)


def sum_kernel(*refs):
    total = refs[0][...].astype(F32)
    for ref in refs[1:-1]:
        total = total + ref[...].astype(F32)
    refs[-1][...] = total.astype(BF16)


def block_sum(terms, count, place):
    shape = (count,) + terms[0].shape[1:]
    return pl.pallas_call(
        sum_kernel,
        grid=(1,),
        out_shape=jax.ShapeDtypeStruct(shape, BF16),
        in_specs=[pl.BlockSpec(shape, lambda i: (place, 0, 0))] * len(terms),
        out_specs=pl.BlockSpec(shape, lambda i: (0, 0, 0)),
        compiler_params=pltpu.CompilerParams(vmem_limit_bytes=16 * 1024 * 1024),
        cost_estimate=CHEAP,
        name="block_sum",
    )(*terms)


def fold_send(terms):
    half = terms[-1].shape[0] // 2
    return block_sum(terms, half, 1)


def fold(terms, bit, frames, send=None):
    send = fold_send(terms) if send is None else send
    return terms + [lax.ppermute(send, "frame", [(i, i ^ (1 << bit)) for i in range(frames)])]


def own_sum(terms):
    return block_sum(terms, 1, 0)[0]


def two_parts(values):
    high = values.astype(BF16).astype(F32)
    zeros = jnp.zeros((10, values.shape[1]), F32)
    return jnp.concatenate([high, values - high, zeros], axis=0).astype(BF16)


def unpack_kernel(terms, last_ref, own_ref, rows_ref):
    share = rows_ref.shape[1]
    own_ref[pl.ds(0, terms), :] = jnp.sum(last_ref[:, pl.ds(0, terms), :].astype(F32), axis=0).astype(BF16)
    gains = jnp.sum(last_ref[:, pl.ds(terms + share, 16), :].astype(F32), axis=0)
    own_ref[pl.ds(terms, 16), :] = two_parts(gains[:3] + gains[3:6])
    rows_ref[...] = last_ref[:, pl.ds(terms, share), :]


def pack_kernel(factor, keep_ref, got_ref, rows_ref, first_ref, second_ref, third_ref, last_ref):
    terms, share = keep_ref.shape[1], rows_ref.shape[1]
    last_ref[:, pl.ds(0, terms), :] = (keep_ref[...].astype(F32) + got_ref[...].astype(F32)).astype(BF16)
    last_ref[:, pl.ds(terms, share), :] = rows_ref[...]
    gains = jnp.concatenate([first_ref[...], second_ref[...], third_ref[...]], axis=0) * factor
    block, width = two_parts(gains), rows_ref.shape[2]
    last_ref[:, pl.ds(terms + share, 16), :] = jnp.broadcast_to(block[None], (keep_ref.shape[0], 16, width))


def finish_kernel(layout, gains, core_ref, own_ref, got_ref, *out_refs):
    if gains is not None:
        pair = [ref[pl.ds(gains, 16), :].astype(F32) for ref in (own_ref, got_ref)]
        out_refs[-1][...] = (pair[0][:3] + pair[0][3:6]) + (pair[1][:3] + pair[1][3:6])

    def store(first_ref, second_ref):
        for half, start, rows, width, out, column in layout:
            piece = (first_ref, second_ref)[half][pl.ds(start, rows), :]
            out_refs[out][:, pl.ds(column, width)] = piece.astype(F32)

    @pl.when(core_ref[0] == 0)
    def _():
        store(own_ref, got_ref)

    @pl.when(core_ref[0] != 0)
    def _():
        store(got_ref, own_ref)


def finish(packed, core, own, got, outs, layout, name, gains=None):
    if packed:
        outs = outs if gains is None else outs + [((3, own.shape[1]), F32)]
        return call(functools.partial(finish_kernel, layout, gains), outs, [core, own, got], scalars=1, vmem=12, name=name)
    pair = jnp.where(core[0] == 0, own, got), jnp.where(core[0] == 0, got, own)
    results = []
    for out in range(len(outs)):
        pieces = [pair[half][start : start + rows] for half, start, rows, _, to, _ in layout if to == out]
        results.append(jnp.concatenate(pieces, axis=1).astype(F32))
    if gains is not None:
        first, second = (x[gains : gains + 6].astype(F32) for x in (own, got))
        results.append((first[:3] + first[3:]) + (second[:3] + second[3:]))
    return results


def exchange(rows, frames):
    blocks = rows.reshape(frames, -1, rows.shape[-1])
    return lax.all_to_all(blocks, "frame", split_axis=0, concat_axis=0, tiled=True)


def body(
    activations,
    cotangent,
    norm_gains,
    time_input,
    time_output,
    space_input,
    space_output,
    hidden_up,
    hidden_down,
):
    frames = lax.axis_size("frame")
    tokens, width = activations.shape[2], activations.shape[3]
    inner = hidden_down.shape[0]
    share = tokens // frames
    packed = share % 16 == 0
    factor = (tokens * frames * lax.axis_size("clip")) ** (-0.5)
    groups = Groups(frames, share)
    group_rows = frames * groups.size
    core = jnp.stack([lax.axis_index("clip"), lax.axis_index("frame")]).astype(jnp.int32)
    rows_bf = ((tokens, width), BF16)
    wide_bf = ((tokens, time_input.shape[1]), BF16)
    gain_f32 = ((1, width), F32)
    if packed:
        attention_terms = [((2 * width, width), BF16)] * 2
        mlp_terms = [((inner, width), BF16)] * 2
    else:
        attention_terms = [(time_input.shape, BF16), (time_output.shape, BF16)]
        mlp_terms = [(hidden_up.shape, BF16), (hidden_down.shape, BF16)]

    def halves(keep, send, folded):
        if packed:
            return [x.reshape(frames, -1, width) for x in (keep, send)]
        return natural_halves(core, frames, folded, keep, send)

    cot = cotangent.reshape(tokens, width)
    patch_rows = exchange(activations.reshape(tokens, width), frames).reshape(tokens, width)
    first_gain_row, time_in, time_out = prefetch(norm_gains, time_input, time_output)
    gain_rows, space_in, space_out = prefetch(norm_gains, space_input, space_output)
    (active_grad,) = call(
        active_grad_kernel, [((tokens, inner), F32)], [cot, hidden_down], vmem=16, name="active_grad", far_in=(0, 1), far_out=(0,)
    )
    first_patch, time_hidden, time_packed, time_mixed, time_shares = call(
        functools.partial(time_forward_kernel, groups),
        [rows_bf, rows_bf, wide_bf, rows_bf, ((width * tokens // HEAD_DIM, group_rows), BF16)],
        [patch_rows, first_gain_row, time_in, time_out],
        vmem=20,
        name="time_forward",
        far_out=(1, 2, 3, 4),
    )
    first_out = exchange(first_patch, frames).reshape(tokens, width)
    second_grad, space_hidden, space_packed, space_mixed, space_shares, third_gain, mlp_keep, mlp_send = call(
        functools.partial(space_mlp_kernel, frames, factor, packed),
        [rows_bf, rows_bf, wide_bf, rows_bf, ((width * tokens // HEAD_DIM, tokens), BF16), gain_f32] + mlp_terms,
        [core, first_out, cot, gain_rows, space_in, space_out, hidden_up, active_grad],
        scalars=1,
        vmem=36,
        name="space_mlp",
        far_in=(2, 6, 7),
        far_out=(1, 3, 5, 6),
    )
    mlp_keep, mlp_send = halves(mlp_keep, mlp_send, True)
    mlp_terms = [mlp_keep, swap_clips(mlp_send)]
    first_grad, space_packed_grad, second_gain = call(
        space_back_kernel,
        [rows_bf, wide_bf, gain_f32],
        [first_out, second_grad, space_packed, space_shares, gain_rows, space_in, space_out],
        vmem=24,
        name="space_back",
        far_out=(1, 2),
    )
    patch_grad = exchange(first_grad, frames).reshape(tokens, width)
    space_keep, space_send = call(
        functools.partial(space_weights_kernel, frames, factor, packed),
        attention_terms,
        [core, space_hidden, space_packed_grad, space_mixed, second_grad],
        scalars=1,
        vmem=20,
        name="space_weights",
        far_in=(1, 2, 3, 4),
        far_out=(0,),
    )
    space_keep, space_send = halves(space_keep, space_send, True)
    bits = fold_bits(frames)
    mlp_send, space_keep, patch_grad = lax.optimization_barrier((fold_send(mlp_terms), space_keep, patch_grad))
    mlp_terms = fold(mlp_terms, bits[0], frames, mlp_send)
    time_packed_grad, time_keep, time_send = call(
        functools.partial(time_back_kernel, groups, factor, packed),
        [wide_bf] + attention_terms,
        [core, patch_grad, time_hidden, time_packed, time_mixed, time_shares, time_output],
        scalars=1,
        scratch=[pltpu.VMEM((tokens, width), BF16)],
        vmem=24,
        name="time_back",
        far_in=(3, 6, 5, 2, 4),
    )
    time_keep, time_send = halves(time_keep, time_send, False)
    time_got = swap_clips(time_send)
    space_terms = [space_keep, swap_clips(space_send)]
    input_patch, first_gain = call(
        time_input_kernel,
        [rows_bf, gain_f32],
        [patch_rows, patch_grad, time_packed_grad, norm_gains, time_input],
        vmem=16,
        name="time_input",
        far_in=(4, 0),
    )
    space_sum, mlp_terms[-1], time_keep = lax.optimization_barrier(
        (fold_send(space_terms), mlp_terms[-1], time_keep)
    )
    space_terms = fold(space_terms, bits[0], frames, space_sum)
    mlp_terms = fold(mlp_terms, bits[1], frames)

    (last,) = call(
        functools.partial(pack_kernel, factor),
        [((frames, 3 * share + 16, width), BF16)],
        [time_keep, time_got, input_patch.reshape(frames, share, width), first_gain, second_gain, third_gain],
        vmem=16,
        name="pack",
        far_out=(0,),
    )
    last = lax.all_to_all(last, "frame", split_axis=0, concat_axis=0, tiled=True)
    late_own, input_grad = call(
        functools.partial(unpack_kernel, 2 * share),
        [((2 * share + 16, width), BF16), ((frames, share, width), BF16)],
        [last],
        vmem=16,
        name="unpack",
    )
    input_grad = input_grad.reshape(activations.shape)

    for bit in bits[1:]:
        space_terms = fold(space_terms, bit, frames)
    for bit in bits[2:]:
        mlp_terms = fold(mlp_terms, bit, frames)
    early_own = jnp.concatenate([own_sum(mlp_terms), own_sum(space_terms)], axis=0)
    early_got = swap_clips(early_own)
    late_got = swap_clips(late_own)

    mlp_rows = inner // frames
    attention_layout = [(0, 0, 0, 0), (0, 1, 0, width), (1, 0, 0, 2 * width), (1, 1, 1, 0)]
    early_layout = [(0, i * share, share, width, 0, i * width) for i in range(inner // width)]
    early_layout += [(1, 0, mlp_rows, width, 1, 0)]
    early_layout += [
        (half, mlp_rows + index * share, share, width, 2 + out, column)
        for half, index, out, column in attention_layout
    ]
    late_layout = [(half, index * share, share, width, out, column) for half, index, out, column in attention_layout]
    attention_outs = [((share, time_input.shape[1]), F32), ((share, width), F32)]
    mlp_outs = [((share, inner), F32), ((mlp_rows, width), F32)]
    up_grad, down_grad, space_in_grad, space_out_grad = finish(
        packed, core, early_own, early_got, mlp_outs + attention_outs, early_layout, "finish_early"
    )
    time_in_grad, time_out_grad, gains_grad = finish(
        packed, core, late_own, late_got, attention_outs, late_layout, "finish_late", gains=2 * share
    )
    return (
        input_grad,
        time_in_grad,
        time_out_grad,
        space_in_grad,
        space_out_grad,
        up_grad,
        down_grad,
        gains_grad,
    )


def solution(mesh):
    tokens = P(("parts", "clip"), "frame", None, None)
    owned = P(("parts", "frame"), None)
    in_specs = (tokens, tokens) + (P(),) * 7
    out_specs = (tokens,) + (owned,) * 6 + (P("parts", None),)
    return jax.shard_map(body, mesh=mesh, in_specs=in_specs, out_specs=out_specs, check_vma=False)
```

time: 150 us -> 127 us (0.85)
  Pallas kernels: 26.4 us -> 44.5 us
  blocking collectives: 17.6 us -> 0 us
  other arithmetic: 15.4 us -> 0.1 us
  local copies, waits for them, and re-layouts: 15 us -> 4.42 us
  starting transfers between devices: 23.2 us -> 33 us
  waiting for transfers between devices: 49.8 us -> 43.1 us
    all_to_all x1, waiting for transfers between devices: 21.9 us -> 0.01 us  [body(): lax.all_to_all(last, 'frame', split_axis=0, concat_axis=0, tiled=True)]
    ppermute x2 -> x6, waiting for transfers between devices: 6.98 us -> 26.5 us  [fold(): lax.ppermute(send, 'frame', [(i, i ^ 1 << bit) for i in range(frames)])]
    pallas_call x6 -> x21, Pallas kernels: 26.4 us -> 44.5 us  [the longest x11 41.3 us: call(): pl.pallas_call(staged, out_shape=[pltpu.HBM(shape, dtype) if i in far_out...]
    all_to_all x1 -> x0, blocking collectives: 17.6 us -> none  [exchange(): lax.all_to_all(blocks, 'frame', split_axis=0, concat_axis=0, tiled=True)]
    all_to_all x2 -> x0, waiting for transfers between devices: 12.1 us -> none  [reduce_by_parity(): lax.all_to_all(mine, 'frame', split_axis=0, concat_axis=0, tiled=True, ax...]
    ppermute x2 -> x6, starting transfers between devices: 2.11 us -> 12.1 us  [fold(): lax.ppermute(send, 'frame', [(i, i ^ 1 << bit) for i in range(frames)])]
    all_to_all x2 -> x0, starting transfers between devices: 9.59 us -> none  [reduce_by_parity(): lax.all_to_all(mine, 'frame', split_axis=0, concat_axis=0, tiled=True, ax...]
    convert_element_type x11 -> x0, other arithmetic: 9.19 us -> none  [the longest x2 4.06 us: reduce_by_parity(): mine = summed(keep[0], got[0], near).astype(BF16)]
  transfers between devices with their start and end apart: 12 -> 15, of which waited for: 4 -> 9; matrix products, arithmetic and copies ran while one was open for 10% -> 0% of each run, Pallas kernels for 10% -> 22%
where the time goes in v2:
time: 127 us; the launch traced here: 126 us
  Pallas kernels  44.5 us (35%)
  waiting for transfers between devices  43.1 us (34%)
  starting transfers between devices  33 us (26%)
  local copies, waits for them, and re-layouts  4.42 us (3%)
    pallas_call x11, Pallas kernels, call(): pl.pallas_call(staged, out_shape=[pltpu.HBM(shape, dtype) if i in far_out...  41.3 us
    ppermute x6, waiting for transfers between devices, fold(): lax.ppermute(send, 'frame', [(i, i ^ 1 << bit) for i in range(frames)])  26.5 us
    all_to_all x3, waiting for transfers between devices, exchange(): lax.all_to_all(blocks, 'frame', split_axis=0, concat_axis=0, tiled=True)  16.6 us
    all_to_all x3, starting transfers between devices, exchange(): lax.all_to_all(blocks, 'frame', split_axis=0, concat_axis=0, tiled=True)  14.7 us
    ppermute x6, starting transfers between devices, fold(): lax.ppermute(send, 'frame', [(i, i ^ 1 << bit) for i in range(frames)])  12.1 us
    all_to_all x1, starting transfers between devices, body(): lax.all_to_all(last, 'frame', split_axis=0, concat_axis=0, tiled=True)  5.12 us
    unnamed x26, local copies, waits for them, and re-layouts  4.42 us
  transfers between devices with their start and end apart: 15, of which 9 were waited for; matrix products, arithmetic and copies ran while one was open for 0% of the time, Pallas kernels for 22%

profile of v2, /device:TPU:0, one launch (start us, length us, event | category | flops | bytes accessed | tf_op | source)
XLA Modules:
  0.0 126.2 jit_solution(6445402484113926278)
XLA Ops:
  0.6 7.3 %all-to-all-start = ((bf16[8,48,384]{2,1,0:T(8,128)(2,1)}), bf16[8,48,384]{2,1,0:T(8,128)(2,1)S(1)}, u32[]{:S(2)}, u32[]{:S(2)}) async-start(bf16[8,48,384]{2,1,0:T(8,128)(2,1)} %bitcast.40), calls=%async_computation | async-start | bytes 589824 | tf_op jit(solution)/shard_map/all_to_all | solution.py:545
  7.9 1.3 %prefetch.2 = (f32[3,384]{1,0:T(4,128)S(1)}, bf16[384,1152]{1,0:T(8,128)(2,1)S(1)}, bf16[384,384]{1,0:T(8,128)(2,1)S(1)}) custom-call(f32[3,384]{1,0:T(4,128)} %refs_3_.1, bf16[384,1152]{1,0:T(8,128)(2,1)} %refs_4_.1, bf16[384,384]{1,0:T(8,128)(2,1)} %refs_6_.3), custom_call_target="tpu_custom_call" | custom-call | flops 1000 | bytes 1000 | tf_op jit(solution)/shard_map/prefetch/pallas_call | solution.py:413
  9.2 8.3 %all-to-all-done = bf16[8,48,384]{2,1,0:T(8,128)(2,1)S(1)} async-done(((bf16[8,48,384]{2,1,0:T(8,128)(2,1)}), bf16[8,48,384]{2,1,0:T(8,128)(2,1)S(1)}, u32[]{:S(2)}, u32[]{:S(2)}) %all-to-all-start) | async-done | bytes 294944 | tf_op jit(solution)/shard_map/all_to_all | solution.py:545
  17.5 3.5 %time_forward.1 = (bf16[384,384]{1,0:T(8,128)(2,1)}, bf16[384,384]{1,0:T(8,128)(2,1)}, bf16[384,1152]{1,0:T(8,128)(2,1)}, bf16[384,384]{1,0:T(8,128)(2,1)}, bf16[2304,128]{1,0:T(8,128)(2,1)}) custom-call(bf16[384,384]{1,0:T(8,128)(2,1)S(1)} %bitcast.29, f32[3,384]{1,0:T(4,128)S(1)} %get-tuple-element.52.refs_1_, ...), custom_call_target="tpu_custom_call" | custom-call | flops 1000 | bytes 1000 | tf_op jit(solution)/shard_map/time_forward/pallas_call | solution.py:388
  21.1 3.6 %all-to-all-start.1 = ((bf16[8,48,384]{2,1,0:T(8,128)(2,1)}), bf16[8,48,384]{2,1,0:T(8,128)(2,1)S(1)}, u32[]{:S(2)}, u32[]{:S(2)}) async-start(bf16[8,48,384]{2,1,0:T(8,128)(2,1)} %bitcast.4), calls=%async_computation.1 | async-start | bytes 589824 | tf_op jit(solution)/shard_map/all_to_all | solution.py:545
  24.7 1.3 %prefetch.3 = (f32[3,384]{1,0:T(4,128)S(1)}, bf16[384,1152]{1,0:T(8,128)(2,1)S(1)}, bf16[384,384]{1,0:T(8,128)(2,1)S(1)}) custom-call(f32[3,384]{1,0:T(4,128)} %refs_3_.1, bf16[384,1152]{1,0:T(8,128)(2,1)} %refs_1_.4, bf16[384,384]{1,0:T(8,128)(2,1)} %refs_2_.3), custom_call_target="tpu_custom_call" | custom-call | flops 1000 | bytes 1000 | tf_op jit(solution)/shard_map/prefetch/pallas_call | solution.py:413
  26.0 3.6 %active_grad.1.refs_7_ = f32[384,1536]{1,0:T(8,128)} custom-call(bf16[384,384]{1,0:T(8,128)(2,1)} %bitcast.38, bf16[1536,384]{1,0:T(8,128)(2,1)} %refs_1_.5), custom_call_target="tpu_custom_call" | custom-call | flops 1000 | bytes 1000 | tf_op jit(solution)/shard_map/active_grad/pallas_call | solution.py:388
  29.7 4.2 %all-to-all-done.1 = bf16[8,48,384]{2,1,0:T(8,128)(2,1)S(1)} async-done(((bf16[8,48,384]{2,1,0:T(8,128)(2,1)}), bf16[8,48,384]{2,1,0:T(8,128)(2,1)S(1)}, u32[]{:S(2)}, u32[]{:S(2)}) %all-to-all-start.1) | async-done | bytes 294944 | tf_op jit(solution)/shard_map/all_to_all | solution.py:545
  33.9 10.3 %space_mlp.1 = (bf16[384,384]{1,0:T(8,128)(2,1)S(1)}, bf16[384,384]{1,0:T(8,128)(2,1)}, bf16[384,1152]{1,0:T(8,128)(2,1)S(1)}, bf16[384,384]{1,0:T(8,128)(2,1)},...) custom-call(s32[2]{0:T(128)S(1)} %pad_add_fusion.refs_0_, ...), custom_call_target="tpu_custom_call" | custom-call | flops 1000 | bytes 1000 | tf_op jit(solution)/shard_map/space_mlp/pallas_call | solution.py:388
  44.3 5.2 %space_back.1 = (bf16[384,384]{1,0:T(8,128)(2,1)}, bf16[384,1152]{1,0:T(8,128)(2,1)}, f32[1,384]{1,0:T(1,128)}) custom-call(bf16[384,384]{1,0:T(8,128)(2,1)S(1)} %bitcast.28, bf16[384,384]{1,0:T(8,128)(2,1)S(1)} %get-tuple-element.62.refs_1_.refs_4_, bf16[384,1152]{1,0:T(8,128)(2,1)S(1)} %get-tuple-element.63.refs_2_, ...), custom_call_target="tpu_custom_call" | custom-call | flops 1000 | bytes 1000 | tf_op jit(solution)/shard_map/space_back/pallas_call | solution.py:388
  49.5 3.8 %all-to-all-start.2 = ((bf16[8,48,384]{2,1,0:T(8,128)(2,1)}), bf16[8,48,384]{2,1,0:T(8,128)(2,1)S(1)}, u32[]{:S(2)}, u32[]{:S(2)}) async-start(bf16[8,48,384]{2,1,0:T(8,128)(2,1)} %bitcast.10), calls=%async_computation.2 | async-start | bytes 589824 | tf_op jit(solution)/shard_map/all_to_all | solution.py:545
  53.3 4.8 %space_weights.1 = (bf16[768,384]{1,0:T(8,128)(2,1)}, bf16[768,384]{1,0:T(8,128)(2,1)}) custom-call(s32[2]{0:T(128)S(1)} %pad_add_fusion.refs_0_, bf16[384,384]{1,0:T(8,128)(2,1)} %get-tuple-element.61.refs_1_, bf16[384,1152]{1,0:T(8,128)(2,1)} %get-tuple-element.65.refs_2_, bf16[384,384]{1,0:T(8,128)(2,1)} %get-tuple-element.66.refs_3_, ...), custom_call_target="tpu_custom_call" | custom-call | flops 1000 | bytes 1000 | tf_op jit(solution)/shard_map/space_weights/pallas_call | solution.py:388
  59.5 4.1 %all-to-all-done.2 = bf16[8,48,384]{2,1,0:T(8,128)(2,1)S(1)} async-done(((bf16[8,48,384]{2,1,0:T(8,128)(2,1)}), bf16[8,48,384]{2,1,0:T(8,128)(2,1)S(1)}, u32[]{:S(2)}, u32[]{:S(2)}) %all-to-all-start.2) | async-done | bytes 294944 | tf_op jit(solution)/shard_map/all_to_all | solution.py:545
  63.6 1.5 %collective-permute-start.2 = (bf16[4,192,384]{2,1,0:T(8,128)(2,1)}, bf16[4,192,384]{2,1,0:T(8,128)(2,1)S(1)}, u32[]{:S(2)}, u32[]{:S(2)}) collective-permute-start(bf16[4,192,384]{2,1,0:T(8,128)(2,1)} %copy-done.8), channel_id=1, source_target_pairs={{0,2},{2,0},{4,6},{6,4},{8,10},{10,8},{12,14},{14,12},{1,3},{3,1},... | collective-permute-start | bytes 1769480 | tf_op jit(solution)/shard_map/ppermute | solution.py:479
  65.0 5.5 %time_back.1 = (bf16[384,1152]{1,0:T(8,128)(2,1)S(1)}, bf16[768,384]{1,0:T(8,128)(2,1)S(1)}, bf16[768,384]{1,0:T(8,128)(2,1)S(1)}) custom-call(s32[2]{0:T(128)S(1)} %pad_add_fusion.refs_0_, bf16[384,384]{1,0:T(8,128)(2,1)S(1)} %bitcast.31, bf16[384,384]{1,0:T(8,128)(2,1)} %get-tuple-element.73.refs_2_, bf16[384,1152]{1,0:T(8,128)(2,1)} %get-tuple-element.74.refs_3_, ...), custom_call_target="tpu_custom_call" | custom-call | flops 1000 | bytes 1000 | tf_op jit(solution)/shard_map/time_back/pallas_call | solution.py:388
  70.7 1.0 copy-done.6
  71.6 2.4 %time_input.1 = (bf16[384,384]{1,0:T(8,128)(2,1)S(1)}, f32[1,384]{1,0:T(1,128)S(1)}) custom-call(bf16[384,384]{1,0:T(8,128)(2,1)} %bitcast.30, bf16[384,384]{1,0:T(8,128)(2,1)S(1)} %bitcast.32, bf16[384,1152]{1,0:T(8,128)(2,1)S(1)} %get-tuple-element.80.refs_2_, f32[3,384]{1,0:T(4,128)S(1)} %copy-done.10, bf16[384,1152]{1,0:T(8,128)(2,1)} %refs_4_.1), custom_call_target="tpu_custom_call" | custom-call | flops 1000 | bytes 1000 | tf_op jit(solution)/shard_map/time_input/pallas_call | solution.py:388
  74.9 2.7 %collective-permute-done.2.refs_2_ = bf16[4,192,384]{2,1,0:T(8,128)(2,1)S(1)} collective-permute-done((bf16[4,192,384]{2,1,0:T(8,128)(2,1)}, bf16[4,192,384]{2,1,0:T(8,128)(2,1)S(1)}, u32[]{:S(2)}, u32[]{:S(2)}) %collective-permute-start.2) | collective-permute-done | bytes 589856 | tf_op jit(solution)/shard_map/ppermute | solution.py:479
  78.4 1.1 pack.1
  79.5 5.1 %all-to-all-start.3 = ((bf16[8,160,384]{2,1,0:T(8,128)(2,1)}), bf16[8,160,384]{2,1,0:T(8,128)(2,1)}, u32[]{:S(2)}, u32[]{:S(2)}) async-start(bf16[8,160,384]{2,1,0:T(8,128)(2,1)} %pack.1), calls=%async_computation.3 | async-start | bytes 1966080 | tf_op jit(solution)/shard_map/all_to_all | solution.py:669
  84.7 2.0 %collective-permute-start.7 = (bf16[4,96,384]{2,1,0:T(8,128)(2,1)}, bf16[4,96,384]{2,1,0:T(8,128)(2,1)S(1)}, u32[]{:S(2)}, u32[]{:S(2)}) collective-permute-start(bf16[4,96,384]{2,1,0:T(8,128)(2,1)} %copy-done.9), channel_id=1, source_target_pairs={{0,2},{2,0},{4,6},{6,4},{8,10},{10,8},{12,14},{14,12},{1,3},{3,1},... | collective-permute-start | bytes 884744 | tf_op jit(solution)/shard_map/ppermute | solution.py:479
  86.7 1.1 copy-done.3
  87.9 1.5 %collective-permute-start.5 = (bf16[2,192,384]{2,1,0:T(8,128)(2,1)S(1)}, bf16[2,192,384]{2,1,0:T(8,128)(2,1)S(1)}, u32[]{:S(2)}, u32[]{:S(2)}) collective-permute-start(bf16[2,192,384]{2,1,0:T(8,128)(2,1)S(1)} %block_sum.10), channel_id=1, source_target_pairs={{0,4},{2,6},{4,0},{6,2},{8,12},{10,14},{12,8},{14,10},{1,5},{3,7},... | collective-permute-start | bytes 884744 | tf_op jit(solution)/shard_map/ppermute | solution.py:479
  89.4 12.6 %collective-permute-done.7.refs_2_ = bf16[4,96,384]{2,1,0:T(8,128)(2,1)S(1)} collective-permute-done((bf16[4,96,384]{2,1,0:T(8,128)(2,1)}, bf16[4,96,384]{2,1,0:T(8,128)(2,1)S(1)}, u32[]{:S(2)}, u32[]{:S(2)}) %collective-permute-start.7) | collective-permute-done | bytes 294944 | tf_op jit(solution)/shard_map/ppermute | solution.py:479
  102.1 1.1 collective-permute-start.8
  103.2 6.9 %collective-permute-done.5.refs_3_ = bf16[2,192,384]{2,1,0:T(8,128)(2,1)S(1)} collective-permute-done((bf16[2,192,384]{2,1,0:T(8,128)(2,1)S(1)}, bf16[2,192,384]{2,1,0:T(8,128)(2,1)S(1)}, u32[]{:S(2)}, u32[]{:S(2)}) %collective-permute-start.5) | collective-permute-done | bytes 294944 | tf_op jit(solution)/shard_map/ppermute | solution.py:479
  110.2 3.0 %collective-permute-start.6 = (bf16[1,192,384]{2,1,0:T(8,128)(2,1)S(1)}, bf16[1,192,384]{2,1,0:T(8,128)(2,1)S(1)}, u32[]{:S(2)}, u32[]{:S(2)}) collective-permute-start(bf16[1,192,384]{2,1,0:T(8,128)(2,1)S(1)} %block_sum.11), channel_id=1, source_target_pairs={{0,8},{2,10},{4,12},{6,14},{8,0},{10,2},{12,4},{14,6},{1,9},{3,11}... | collective-permute-start | bytes 442376 | tf_op jit(solution)/shard_map/ppermute | solution.py:479
  113.3 3.0 %collective-permute-start.9 = (bf16[1,96,384]{2,1,0:T(8,128)(2,1)S(1)}, bf16[1,96,384]{2,1,0:T(8,128)(2,1)S(1)}, u32[]{:S(2)}, u32[]{:S(2)}) collective-permute-start(bf16[1,96,384]{2,1,0:T(8,128)(2,1)S(1)} %block_sum.14), channel_id=1, source_target_pairs={{0,8},{2,10},{4,12},{6,14},{8,0},{10,2},{12,4},{14,6},{1,9},{3,11}... | collective-permute-start | bytes 221192 | tf_op jit(solution)/shard_map/ppermute | solution.py:479
  116.3 3.4 %collective-permute-done.6.refs_4_ = bf16[1,192,384]{2,1,0:T(8,128)(2,1)S(1)} collective-permute-done((bf16[1,192,384]{2,1,0:T(8,128)(2,1)S(1)}, bf16[1,192,384]{2,1,0:T(8,128)(2,1)S(1)}, u32[]{:S(2)}, u32[]{:S(2)}) %collective-permute-start.6) | collective-permute-done | bytes 147488 | tf_op jit(solution)/shard_map/ppermute | solution.py:479
  120.7 1.9 %unpack.1 = (bf16[112,384]{1,0:T(8,128)(2,1)S(1)}, bf16[8,48,384]{2,1,0:T(8,128)(2,1)}) custom-call(bf16[8,160,384]{2,1,0:T(8,128)(2,1)} %all-to-all-done.3.refs_0_), custom_call_target="tpu_custom_call" | custom-call | flops 1000 | bytes 1000 | tf_op jit(solution)/shard_map/unpack/pallas_call | solution.py:388
  123.2 1.5 %finish_early.1 = (f32[48,1536]{1,0:T(8,128)}, f32[192,384]{1,0:T(8,128)}, f32[48,1152]{1,0:T(8,128)}, f32[48,384]{1,0:T(8,128)}) custom-call(s32[2]{0:T(128)S(1)} %pad_add_fusion.refs_0_, bf16[288,384]{1,0:T(8,128)(2,1)S(1)} %pad_maximum_fusion.refs_1_, bf16[288,384]{1,0:T(8,128)(2,1)S(1)} %collective-permute-done.10.refs_2_), custom_call_target="tpu_custom_call" | custom-call | flops 1000 | bytes 1000 | tf_op jit(solution)/shard_map/finish_early/pallas_call | solution.py:388
  124.7 1.3 %finish_late.1 = (f32[48,1152]{1,0:T(8,128)}, f32[48,384]{1,0:T(8,128)}, f32[3,384]{1,0:T(4,128)}) custom-call(s32[2]{0:T(128)S(1)} %pad_add_fusion.refs_0_, bf16[112,384]{1,0:T(8,128)(2,1)S(1)} %get-tuple-element.86.refs_1_, bf16[112,384]{1,0:T(8,128)(2,1)S(1)} %collective-permute-done.4.refs_2_), custom_call_target="tpu_custom_call" | custom-call | flops 1000 | bytes 1000 | tf_op jit(solution)/shard_map/finish_late/pallas_call | solution.py:388
  (47 shorter events, 5.1 us)
Async XLA Ops:
  0.6 16.9 %all-to-all-start = ((bf16[8,48,384]{2,1,0:T(8,128)(2,1)}), bf16[8,48,384]{2,1,0:T(8,128)(2,1)S(1)}, u32[]{:S(2)}, u32[]{:S(2)}) async-start(bf16[8,48,384]{2,1,0:T(8,128)(2,1)} %bitcast.40), calls=%async_computation | async-start | bytes 589824 | tf_op jit(solution)/shard_map/all_to_all | solution.py:545
  17.5 3.5 %copy-start.4 = (bf16[8,48,384]{2,1,0:T(8,128)(2,1)}, bf16[8,48,384]{2,1,0:T(8,128)(2,1)S(1)}, u32[]{:S(2)}) copy-start(bf16[8,48,384]{2,1,0:T(8,128)(2,1)S(1)} %all-to-all-done) | copy-start | bytes 884740
  21.1 12.8 %all-to-all-start.1 = ((bf16[8,48,384]{2,1,0:T(8,128)(2,1)}), bf16[8,48,384]{2,1,0:T(8,128)(2,1)S(1)}, u32[]{:S(2)}, u32[]{:S(2)}) async-start(bf16[8,48,384]{2,1,0:T(8,128)(2,1)} %bitcast.4), calls=%async_computation.1 | async-start | bytes 589824 | tf_op jit(solution)/shard_map/all_to_all | solution.py:545
  44.2 5.3 %copy-start.7 = (bf16[384,384]{1,0:T(8,128)(2,1)}, bf16[384,384]{1,0:T(8,128)(2,1)S(1)}, u32[]{:S(2)}) copy-start(bf16[384,384]{1,0:T(8,128)(2,1)S(1)} %get-tuple-element.62.refs_1_.refs_4_) | copy-start | bytes 884740
  44.2 14.3 %collective-permute-start = (bf16[8,192,384]{2,1,0:T(8,128)(2,1)}, bf16[8,192,384]{2,1,0:T(8,128)(2,1)S(1)}, u32[]{:S(2)}, u32[]{:S(2)}) collective-permute-start(bf16[8,192,384]{2,1,0:T(8,128)(2,1)} %bitcast.8), channel_id=1, source_target_pairs={{0,1},{1,0},{2,3},{3,2},{4,5},{5,4},{6,7},{7,6},{8,9},{9,8},{10,11... | collective-permute-start | bytes 3538952 | tf_op jit(solution)/shard_map/ppermute | solution.py:445
  49.5 9.0 %copy-start = (bf16[1536,384]{1,0:T(8,128)(2,1)S(1)}, bf16[1536,384]{1,0:T(8,128)(2,1)}, u32[]{:S(2)}) copy-start(bf16[1536,384]{1,0:T(8,128)(2,1)} %get-tuple-element.59) | copy-start | bytes 3538948
  49.5 14.0 %all-to-all-start.2 = ((bf16[8,48,384]{2,1,0:T(8,128)(2,1)}), bf16[8,48,384]{2,1,0:T(8,128)(2,1)S(1)}, u32[]{:S(2)}, u32[]{:S(2)}) async-start(bf16[8,48,384]{2,1,0:T(8,128)(2,1)} %bitcast.10), calls=%async_computation.2 | async-start | bytes 589824 | tf_op jit(solution)/shard_map/all_to_all | solution.py:545
  58.2 15.9 %collective-permute-start.1 = (bf16[8,96,384]{2,1,0:T(8,128)(2,1)}, bf16[8,96,384]{2,1,0:T(8,128)(2,1)S(1)}, u32[]{:S(2)}, u32[]{:S(2)}) collective-permute-start(bf16[8,96,384]{2,1,0:T(8,128)(2,1)} %bitcast.12), channel_id=1, source_target_pairs={{0,1},{1,0},{2,3},{3,2},{4,5},{5,4},{6,7},{7,6},{8,9},{9,8},{10,11... | collective-permute-start | bytes 1769480 | tf_op jit(solution)/shard_map/ppermute | solution.py:445
  58.7 0.8 copy-start.8
  63.6 7.0 %copy-start.5 = (bf16[8,48,384]{2,1,0:T(8,128)(2,1)}, bf16[8,48,384]{2,1,0:T(8,128)(2,1)S(1)}, u32[]{:S(2)}) copy-start(bf16[8,48,384]{2,1,0:T(8,128)(2,1)S(1)} %all-to-all-done.2) | copy-start | bytes 884740
  63.6 14.0 %collective-permute-start.2 = (bf16[4,192,384]{2,1,0:T(8,128)(2,1)}, bf16[4,192,384]{2,1,0:T(8,128)(2,1)S(1)}, u32[]{:S(2)}, u32[]{:S(2)}) collective-permute-start(bf16[4,192,384]{2,1,0:T(8,128)(2,1)} %copy-done.8), channel_id=1, source_target_pairs={{0,2},{2,0},{4,6},{6,4},{8,10},{10,8},{12,14},{14,12},{1,3},{3,1},... | collective-permute-start | bytes 1769480 | tf_op jit(solution)/shard_map/ppermute | solution.py:479
  65.0 5.6 %copy-start.10 = (f32[3,384]{1,0:T(4,128)S(1)}, f32[3,384]{1,0:T(4,128)}, u32[]{:S(2)}) copy-start(f32[3,384]{1,0:T(4,128)} %refs_3_.1) | copy-start | bytes 13828
  70.6 7.8 %collective-permute-start.3 = (bf16[8,96,384]{2,1,0:T(8,128)(2,1)S(1)}, bf16[8,96,384]{2,1,0:T(8,128)(2,1)S(1)}, u32[]{:S(2)}, u32[]{:S(2)}) collective-permute-start(bf16[8,96,384]{2,1,0:T(8,128)(2,1)S(1)} %bitcast.37), channel_id=1, source_target_pairs={{0,1},{1,0},{2,3},{3,2},{4,5},{5,4},{6,7},{7,6},{8,9},{9,8},{10,11... | collective-permute-start | bytes 1769480 | tf_op jit(solution)/shard_map/ppermute | solution.py:445
  70.7 1.0 copy-start.6
  71.6 2.4 %copy-start.1 = (bf16[768,384]{1,0:T(8,128)(2,1)S(1)}, bf16[768,384]{1,0:T(8,128)(2,1)}, u32[]{:S(2)}) copy-start(bf16[768,384]{1,0:T(8,128)(2,1)} %get-tuple-element.67) | copy-start | bytes 1769476
  74.0 4.4 %copy-start.11 = (f32[1,384]{1,0:T(1,128)S(1)}, f32[1,384]{1,0:T(1,128)}, u32[]{:S(2)}) copy-start(f32[1,384]{1,0:T(1,128)} %get-tuple-element.84.refs_5_) | copy-start | bytes 4612
  74.0 4.4 %copy-start.12 = (f32[1,384]{1,0:T(1,128)S(1)}, f32[1,384]{1,0:T(1,128)}, u32[]{:S(2)}) copy-start(f32[1,384]{1,0:T(1,128)} %get-tuple-element.83.refs_4_) | copy-start | bytes 4612
  74.2 0.7 copy-start.9
  77.6 0.8 copy-start.2
  79.5 41.1 %all-to-all-start.3 = ((bf16[8,160,384]{2,1,0:T(8,128)(2,1)}), bf16[8,160,384]{2,1,0:T(8,128)(2,1)}, u32[]{:S(2)}, u32[]{:S(2)}) async-start(bf16[8,160,384]{2,1,0:T(8,128)(2,1)} %pack.1), calls=%async_computation.3 | async-start | bytes 1966080 | tf_op jit(solution)/shard_map/all_to_all | solution.py:669
  84.7 17.3 %collective-permute-start.7 = (bf16[4,96,384]{2,1,0:T(8,128)(2,1)}, bf16[4,96,384]{2,1,0:T(8,128)(2,1)S(1)}, u32[]{:S(2)}, u32[]{:S(2)}) collective-permute-start(bf16[4,96,384]{2,1,0:T(8,128)(2,1)} %copy-done.9), channel_id=1, source_target_pairs={{0,2},{2,0},{4,6},{6,4},{8,10},{10,8},{12,14},{14,12},{1,3},{3,1},... | collective-permute-start | bytes 884744 | tf_op jit(solution)/shard_map/ppermute | solution.py:479
  86.7 1.1 copy-start.3
  87.9 22.3 %collective-permute-start.5 = (bf16[2,192,384]{2,1,0:T(8,128)(2,1)S(1)}, bf16[2,192,384]{2,1,0:T(8,128)(2,1)S(1)}, u32[]{:S(2)}, u32[]{:S(2)}) collective-permute-start(bf16[2,192,384]{2,1,0:T(8,128)(2,1)S(1)} %block_sum.10), channel_id=1, source_target_pairs={{0,4},{2,6},{4,0},{6,2},{8,12},{10,14},{12,8},{14,10},{1,5},{3,7},... | collective-permute-start | bytes 884744 | tf_op jit(solution)/shard_map/ppermute | solution.py:479
  102.1 11.2 %collective-permute-start.8 = (bf16[2,96,384]{2,1,0:T(8,128)(2,1)S(1)}, bf16[2,96,384]{2,1,0:T(8,128)(2,1)S(1)}, u32[]{:S(2)}, u32[]{:S(2)}) collective-permute-start(bf16[2,96,384]{2,1,0:T(8,128)(2,1)S(1)} %block_sum.13), channel_id=1, source_target_pairs={{0,4},{2,6},{4,0},{6,2},{8,12},{10,14},{12,8},{14,10},{1,5},{3,7},... | collective-permute-start | bytes 442376 | tf_op jit(solution)/shard_map/ppermute | solution.py:479
  110.2 9.5 %collective-permute-start.6 = (bf16[1,192,384]{2,1,0:T(8,128)(2,1)S(1)}, bf16[1,192,384]{2,1,0:T(8,128)(2,1)S(1)}, u32[]{:S(2)}, u32[]{:S(2)}) collective-permute-start(bf16[1,192,384]{2,1,0:T(8,128)(2,1)S(1)} %block_sum.11), channel_id=1, source_target_pairs={{0,8},{2,10},{4,12},{6,14},{8,0},{10,2},{12,4},{14,6},{1,9},{3,11}... | collective-permute-start | bytes 442376 | tf_op jit(solution)/shard_map/ppermute | solution.py:479
  113.3 7.1 %collective-permute-start.9 = (bf16[1,96,384]{2,1,0:T(8,128)(2,1)S(1)}, bf16[1,96,384]{2,1,0:T(8,128)(2,1)S(1)}, u32[]{:S(2)}, u32[]{:S(2)}) collective-permute-start(bf16[1,96,384]{2,1,0:T(8,128)(2,1)S(1)} %block_sum.14), channel_id=1, source_target_pairs={{0,8},{2,10},{4,12},{6,14},{8,0},{10,2},{12,4},{14,6},{1,9},{3,11}... | collective-permute-start | bytes 221192 | tf_op jit(solution)/shard_map/ppermute | solution.py:479
  120.6 2.6 %collective-permute-start.10 = (bf16[288,384]{1,0:T(8,128)(2,1)S(1)}, bf16[288,384]{1,0:T(8,128)(2,1)S(1)}, u32[]{:S(2)}, u32[]{:S(2)}) collective-permute-start(bf16[288,384]{1,0:T(8,128)(2,1)S(1)} %pad_maximum_fusion.refs_1_), channel_id=1, source_target_pairs={{0,1},{1,0},{2,3},{3,2},{4,5},{5,4},{6,7},{7,6},{8,9},{9,8},{10,11... | collective-permute-start | bytes 663560 | tf_op jit(solution)/shard_map/ppermute | solution.py:445
  122.6 2.1 %collective-permute-start.4 = (bf16[112,384]{1,0:T(8,128)(2,1)S(1)}, bf16[112,384]{1,0:T(8,128)(2,1)S(1)}, u32[]{:S(2)}, u32[]{:S(2)}) collective-permute-start(bf16[112,384]{1,0:T(8,128)(2,1)S(1)} %get-tuple-element.86.refs_1_), channel_id=1, source_target_pairs={{0,1},{1,0},{2,3},{3,2},{4,5},{5,4},{6,7},{7,6},{8,9},{9,8},{10,11... | collective-permute-start | bytes 258056 | tf_op jit(solution)/shard_map/ppermute | solution.py:445

commit v3 on v2

--- a/solution.py
+++ b/solution.py
@@ -135,6 +135,7 @@
     hidden = (normed * gains_ref[0:1, :]).astype(BF16)
     hidden_ref[...] = hidden
     packed_ref[...] = nn(hidden, in_ref[...]).astype(BF16)
+    send(hidden_ref, packed_ref)
     mask = groups.mask()
     block = 0
     for group in range(groups.count):
@@ -144,7 +145,7 @@
             groups.store(mixed_ref, group, first, mixed)
             shares_ref[pl.ds(block, shares.shape[0]), :] = shares
             block += shares.shape[0]
-    send(hidden_ref, packed_ref, mixed_ref, shares_ref)
+    send(mixed_ref, shares_ref)
     first_ref[...] = (rows + nn(mixed_ref[...], out_ref[...])).astype(BF16)
 
 
@@ -604,7 +605,7 @@
         vmem=36,
         name="space_mlp",
         far_in=(2, 6, 7),
-        far_out=(1, 3, 5, 6),
+        far_out=(1, 3, 5),
     )
     mlp_keep, mlp_send = halves(mlp_keep, mlp_send, True)
     mlp_terms = [mlp_keep, swap_clips(mlp_send)]

time: 127 us -> 127 us (level)
  local copies, waits for them, and re-layouts: 4.42 us -> 6.11 us
  Pallas kernels: 44.5 us -> 42.9 us
    unnamed x26 -> x30, local copies, waits for them, and re-layouts: 4.42 us -> 6.11 us
    pallas_call x11, Pallas kernels: 41.3 us -> 39.7 us  [call(): pl.pallas_call(staged, out_shape=[pltpu.HBM(shape, dtype) if i in far_out...]
where the time goes in v3:
time: 127 us; the launch traced here: 126 us
  Pallas kernels  42.9 us (34%)
  waiting for transfers between devices  42.9 us (34%)
  starting transfers between devices  32.8 us (26%)
  local copies, waits for them, and re-layouts  6.11 us (5%)
    pallas_call x11, Pallas kernels, call(): pl.pallas_call(staged, out_shape=[pltpu.HBM(shape, dtype) if i in far_out...  39.7 us
    ppermute x6, waiting for transfers between devices, fold(): lax.ppermute(send, 'frame', [(i, i ^ 1 << bit) for i in range(frames)])  26.4 us
    all_to_all x3, waiting for transfers between devices, exchange(): lax.all_to_all(blocks, 'frame', split_axis=0, concat_axis=0, tiled=True)  16.4 us
    all_to_all x3, starting transfers between devices, exchange(): lax.all_to_all(blocks, 'frame', split_axis=0, concat_axis=0, tiled=True)  14.5 us
    ppermute x6, starting transfers between devices, fold(): lax.ppermute(send, 'frame', [(i, i ^ 1 << bit) for i in range(frames)])  12.1 us
    unnamed x30, local copies, waits for them, and re-layouts  6.11 us
    all_to_all x1, starting transfers between devices, body(): lax.all_to_all(last, 'frame', split_axis=0, concat_axis=0, tiled=True)  5.11 us
  transfers between devices with their start and end apart: 15, of which 9 were waited for; matrix products, arithmetic and copies ran while one was open for 0% of the time, Pallas kernels for 22%

profile of v3, /device:TPU:0, one launch (start us, length us, event | category | flops | bytes accessed | tf_op | source)
XLA Modules:
  0.0 125.9 jit_solution(8748044995859432284)
XLA Ops:
  0.6 7.3 %all-to-all-start = ((bf16[8,48,384]{2,1,0:T(8,128)(2,1)}), bf16[8,48,384]{2,1,0:T(8,128)(2,1)S(1)}, u32[]{:S(2)}, u32[]{:S(2)}) async-start(bf16[8,48,384]{2,1,0:T(8,128)(2,1)} %bitcast.41), calls=%async_computation | async-start | bytes 589824 | tf_op jit(solution)/shard_map/all_to_all | solution.py:546
  7.9 1.3 %prefetch.2 = (f32[3,384]{1,0:T(4,128)S(1)}, bf16[384,1152]{1,0:T(8,128)(2,1)S(1)}, bf16[384,384]{1,0:T(8,128)(2,1)S(1)}) custom-call(f32[3,384]{1,0:T(4,128)} %refs_3_.1, bf16[384,1152]{1,0:T(8,128)(2,1)} %refs_4_.1, bf16[384,384]{1,0:T(8,128)(2,1)} %refs_6_.3), custom_call_target="tpu_custom_call" | custom-call | flops 1000 | bytes 1000 | tf_op jit(solution)/shard_map/prefetch/pallas_call | solution.py:414
  9.2 8.3 %all-to-all-done = bf16[8,48,384]{2,1,0:T(8,128)(2,1)S(1)} async-done(((bf16[8,48,384]{2,1,0:T(8,128)(2,1)}), bf16[8,48,384]{2,1,0:T(8,128)(2,1)S(1)}, u32[]{:S(2)}, u32[]{:S(2)}) %all-to-all-start) | async-done | bytes 294944 | tf_op jit(solution)/shard_map/all_to_all | solution.py:546
  17.5 3.5 %time_forward.1 = (bf16[384,384]{1,0:T(8,128)(2,1)}, bf16[384,384]{1,0:T(8,128)(2,1)}, bf16[384,1152]{1,0:T(8,128)(2,1)}, bf16[384,384]{1,0:T(8,128)(2,1)}, bf16[2304,128]{1,0:T(8,128)(2,1)}) custom-call(bf16[384,384]{1,0:T(8,128)(2,1)S(1)} %bitcast.29, f32[3,384]{1,0:T(4,128)S(1)} %get-tuple-element.52.refs_1_, ...), custom_call_target="tpu_custom_call" | custom-call | flops 1000 | bytes 1000 | tf_op jit(solution)/shard_map/time_forward/pallas_call | solution.py:389
  21.1 3.6 %all-to-all-start.1 = ((bf16[8,48,384]{2,1,0:T(8,128)(2,1)}), bf16[8,48,384]{2,1,0:T(8,128)(2,1)S(1)}, u32[]{:S(2)}, u32[]{:S(2)}) async-start(bf16[8,48,384]{2,1,0:T(8,128)(2,1)} %bitcast.4), calls=%async_computation.1 | async-start | bytes 589824 | tf_op jit(solution)/shard_map/all_to_all | solution.py:546
  24.7 1.3 %prefetch.3 = (f32[3,384]{1,0:T(4,128)S(1)}, bf16[384,1152]{1,0:T(8,128)(2,1)S(1)}, bf16[384,384]{1,0:T(8,128)(2,1)S(1)}) custom-call(f32[3,384]{1,0:T(4,128)} %refs_3_.1, bf16[384,1152]{1,0:T(8,128)(2,1)} %refs_1_.4, bf16[384,384]{1,0:T(8,128)(2,1)} %refs_2_.3), custom_call_target="tpu_custom_call" | custom-call | flops 1000 | bytes 1000 | tf_op jit(solution)/shard_map/prefetch/pallas_call | solution.py:414
  26.0 3.7 %active_grad.1.refs_7_ = f32[384,1536]{1,0:T(8,128)} custom-call(bf16[384,384]{1,0:T(8,128)(2,1)} %bitcast.39, bf16[1536,384]{1,0:T(8,128)(2,1)} %refs_1_.5), custom_call_target="tpu_custom_call" | custom-call | flops 1000 | bytes 1000 | tf_op jit(solution)/shard_map/active_grad/pallas_call | solution.py:389
  29.8 4.1 %all-to-all-done.1 = bf16[8,48,384]{2,1,0:T(8,128)(2,1)S(1)} async-done(((bf16[8,48,384]{2,1,0:T(8,128)(2,1)}), bf16[8,48,384]{2,1,0:T(8,128)(2,1)S(1)}, u32[]{:S(2)}, u32[]{:S(2)}) %all-to-all-start.1) | async-done | bytes 294944 | tf_op jit(solution)/shard_map/all_to_all | solution.py:546
  33.9 9.3 %space_mlp.1 = (bf16[384,384]{1,0:T(8,128)(2,1)S(1)}, bf16[384,384]{1,0:T(8,128)(2,1)}, bf16[384,1152]{1,0:T(8,128)(2,1)S(1)}, bf16[384,384]{1,0:T(8,128)(2,1)},...) custom-call(s32[2]{0:T(128)S(1)} %pad_add_fusion.refs_0_, ...), custom_call_target="tpu_custom_call" | custom-call | flops 1000 | bytes 1000 | tf_op jit(solution)/shard_map/space_mlp/pallas_call | solution.py:389
  43.3 1.0 copy-done.7
  44.3 4.5 %space_back.1 = (bf16[384,384]{1,0:T(8,128)(2,1)S(1)}, bf16[384,1152]{1,0:T(8,128)(2,1)}, f32[1,384]{1,0:T(1,128)}) custom-call(bf16[384,384]{1,0:T(8,128)(2,1)S(1)} %bitcast.28, bf16[384,384]{1,0:T(8,128)(2,1)S(1)} %get-tuple-element.62.refs_1_.refs_4_, bf16[384,1152]{1,0:T(8,128)(2,1)S(1)} %get-tuple-element.63.refs_2_, ...), custom_call_target="tpu_custom_call" | custom-call | flops 1000 | bytes 1000 | tf_op jit(solution)/shard_map/space_back/pallas_call | solution.py:389
  49.5 3.6 %all-to-all-start.2 = ((bf16[8,48,384]{2,1,0:T(8,128)(2,1)}), bf16[8,48,384]{2,1,0:T(8,128)(2,1)S(1)}, u32[]{:S(2)}, u32[]{:S(2)}) async-start(bf16[8,48,384]{2,1,0:T(8,128)(2,1)} %bitcast.36), calls=%async_computation.2 | async-start | bytes 589824 | tf_op jit(solution)/shard_map/all_to_all | solution.py:546
  53.1 4.9 %space_weights.1 = (bf16[768,384]{1,0:T(8,128)(2,1)}, bf16[768,384]{1,0:T(8,128)(2,1)}) custom-call(s32[2]{0:T(128)S(1)} %pad_add_fusion.refs_0_, bf16[384,384]{1,0:T(8,128)(2,1)} %get-tuple-element.61.refs_1_, bf16[384,1152]{1,0:T(8,128)(2,1)} %get-tuple-element.65.refs_2_, bf16[384,384]{1,0:T(8,128)(2,1)} %get-tuple-element.66.refs_3_, ...), custom_call_target="tpu_custom_call" | custom-call | flops 1000 | bytes 1000 | tf_op jit(solution)/shard_map/space_weights/pallas_call | solution.py:389
  59.3 4.0 %all-to-all-done.2 = bf16[8,48,384]{2,1,0:T(8,128)(2,1)S(1)} async-done(((bf16[8,48,384]{2,1,0:T(8,128)(2,1)}), bf16[8,48,384]{2,1,0:T(8,128)(2,1)S(1)}, u32[]{:S(2)}, u32[]{:S(2)}) %all-to-all-start.2) | async-done | bytes 294944 | tf_op jit(solution)/shard_map/all_to_all | solution.py:546
  63.3 1.5 %collective-permute-start.2 = (bf16[4,192,384]{2,1,0:T(8,128)(2,1)}, bf16[4,192,384]{2,1,0:T(8,128)(2,1)S(1)}, u32[]{:S(2)}, u32[]{:S(2)}) collective-permute-start(bf16[4,192,384]{2,1,0:T(8,128)(2,1)} %copy-done.9), channel_id=1, source_target_pairs={{0,2},{2,0},{4,6},{6,4},{8,10},{10,8},{12,14},{14,12},{1,3},{3,1},... | collective-permute-start | bytes 1769480 | tf_op jit(solution)/shard_map/ppermute | solution.py:480
  64.8 5.5 %time_back.1 = (bf16[384,1152]{1,0:T(8,128)(2,1)S(1)}, bf16[768,384]{1,0:T(8,128)(2,1)S(1)}, bf16[768,384]{1,0:T(8,128)(2,1)S(1)}) custom-call(s32[2]{0:T(128)S(1)} %pad_add_fusion.refs_0_, bf16[384,384]{1,0:T(8,128)(2,1)S(1)} %bitcast.31, bf16[384,384]{1,0:T(8,128)(2,1)} %get-tuple-element.73.refs_2_, bf16[384,1152]{1,0:T(8,128)(2,1)} %get-tuple-element.74.refs_3_, ...), custom_call_target="tpu_custom_call" | custom-call | flops 1000 | bytes 1000 | tf_op jit(solution)/shard_map/time_back/pallas_call | solution.py:389
  71.4 2.4 %time_input.1 = (bf16[384,384]{1,0:T(8,128)(2,1)S(1)}, f32[1,384]{1,0:T(1,128)S(1)}) custom-call(bf16[384,384]{1,0:T(8,128)(2,1)} %bitcast.30, bf16[384,384]{1,0:T(8,128)(2,1)S(1)} %bitcast.32, bf16[384,1152]{1,0:T(8,128)(2,1)S(1)} %get-tuple-element.80.refs_2_, f32[3,384]{1,0:T(4,128)S(1)} %copy-done.12, bf16[384,1152]{1,0:T(8,128)(2,1)} %refs_4_.1), custom_call_target="tpu_custom_call" | custom-call | flops 1000 | bytes 1000 | tf_op jit(solution)/shard_map/time_input/pallas_call | solution.py:389
  74.7 2.7 %collective-permute-done.2.refs_2_ = bf16[4,192,384]{2,1,0:T(8,128)(2,1)S(1)} collective-permute-done((bf16[4,192,384]{2,1,0:T(8,128)(2,1)}, bf16[4,192,384]{2,1,0:T(8,128)(2,1)S(1)}, u32[]{:S(2)}, u32[]{:S(2)}) %collective-permute-start.2) | collective-permute-done | bytes 589856 | tf_op jit(solution)/shard_map/ppermute | solution.py:480
  78.2 1.1 pack.1
  79.3 5.1 %all-to-all-start.3 = ((bf16[8,160,384]{2,1,0:T(8,128)(2,1)}), bf16[8,160,384]{2,1,0:T(8,128)(2,1)}, u32[]{:S(2)}, u32[]{:S(2)}) async-start(bf16[8,160,384]{2,1,0:T(8,128)(2,1)} %pack.1), calls=%async_computation.3 | async-start | bytes 1966080 | tf_op jit(solution)/shard_map/all_to_all | solution.py:670
  84.4 2.0 %collective-permute-start.7 = (bf16[4,96,384]{2,1,0:T(8,128)(2,1)}, bf16[4,96,384]{2,1,0:T(8,128)(2,1)S(1)}, u32[]{:S(2)}, u32[]{:S(2)}) collective-permute-start(bf16[4,96,384]{2,1,0:T(8,128)(2,1)} %copy-done.11), channel_id=1, source_target_pairs={{0,2},{2,0},{4,6},{6,4},{8,10},{10,8},{12,14},{14,12},{1,3},{3,1},... | collective-permute-start | bytes 884744 | tf_op jit(solution)/shard_map/ppermute | solution.py:480
  86.4 1.1 copy-done.2
  87.6 1.5 %collective-permute-start.5 = (bf16[2,192,384]{2,1,0:T(8,128)(2,1)S(1)}, bf16[2,192,384]{2,1,0:T(8,128)(2,1)S(1)}, u32[]{:S(2)}, u32[]{:S(2)}) collective-permute-start(bf16[2,192,384]{2,1,0:T(8,128)(2,1)S(1)} %block_sum.10), channel_id=1, source_target_pairs={{0,4},{2,6},{4,0},{6,2},{8,12},{10,14},{12,8},{14,10},{1,5},{3,7},... | collective-permute-start | bytes 884744 | tf_op jit(solution)/shard_map/ppermute | solution.py:480
  89.1 12.6 %collective-permute-done.7.refs_2_ = bf16[4,96,384]{2,1,0:T(8,128)(2,1)S(1)} collective-permute-done((bf16[4,96,384]{2,1,0:T(8,128)(2,1)}, bf16[4,96,384]{2,1,0:T(8,128)(2,1)S(1)}, u32[]{:S(2)}, u32[]{:S(2)}) %collective-permute-start.7) | collective-permute-done | bytes 294944 | tf_op jit(solution)/shard_map/ppermute | solution.py:480
  101.8 1.1 collective-permute-start.8
  102.9 6.9 %collective-permute-done.5.refs_3_ = bf16[2,192,384]{2,1,0:T(8,128)(2,1)S(1)} collective-permute-done((bf16[2,192,384]{2,1,0:T(8,128)(2,1)S(1)}, bf16[2,192,384]{2,1,0:T(8,128)(2,1)S(1)}, u32[]{:S(2)}, u32[]{:S(2)}) %collective-permute-start.5) | collective-permute-done | bytes 294944 | tf_op jit(solution)/shard_map/ppermute | solution.py:480
  110.0 3.0 %collective-permute-start.6 = (bf16[1,192,384]{2,1,0:T(8,128)(2,1)S(1)}, bf16[1,192,384]{2,1,0:T(8,128)(2,1)S(1)}, u32[]{:S(2)}, u32[]{:S(2)}) collective-permute-start(bf16[1,192,384]{2,1,0:T(8,128)(2,1)S(1)} %block_sum.11), channel_id=1, source_target_pairs={{0,8},{2,10},{4,12},{6,14},{8,0},{10,2},{12,4},{14,6},{1,9},{3,11}... | collective-permute-start | bytes 442376 | tf_op jit(solution)/shard_map/ppermute | solution.py:480
  113.1 3.0 %collective-permute-start.9 = (bf16[1,96,384]{2,1,0:T(8,128)(2,1)S(1)}, bf16[1,96,384]{2,1,0:T(8,128)(2,1)S(1)}, u32[]{:S(2)}, u32[]{:S(2)}) collective-permute-start(bf16[1,96,384]{2,1,0:T(8,128)(2,1)S(1)} %block_sum.14), channel_id=1, source_target_pairs={{0,8},{2,10},{4,12},{6,14},{8,0},{10,2},{12,4},{14,6},{1,9},{3,11}... | collective-permute-start | bytes 221192 | tf_op jit(solution)/shard_map/ppermute | solution.py:480
  116.0 3.4 %collective-permute-done.6.refs_4_ = bf16[1,192,384]{2,1,0:T(8,128)(2,1)S(1)} collective-permute-done((bf16[1,192,384]{2,1,0:T(8,128)(2,1)S(1)}, bf16[1,192,384]{2,1,0:T(8,128)(2,1)S(1)}, u32[]{:S(2)}, u32[]{:S(2)}) %collective-permute-start.6) | collective-permute-done | bytes 147488 | tf_op jit(solution)/shard_map/ppermute | solution.py:480
  120.4 1.9 %unpack.1 = (bf16[112,384]{1,0:T(8,128)(2,1)S(1)}, bf16[8,48,384]{2,1,0:T(8,128)(2,1)}) custom-call(bf16[8,160,384]{2,1,0:T(8,128)(2,1)} %all-to-all-done.3.refs_0_), custom_call_target="tpu_custom_call" | custom-call | flops 1000 | bytes 1000 | tf_op jit(solution)/shard_map/unpack/pallas_call | solution.py:389
  122.9 1.5 %finish_early.1 = (f32[48,1536]{1,0:T(8,128)}, f32[192,384]{1,0:T(8,128)}, f32[48,1152]{1,0:T(8,128)}, f32[48,384]{1,0:T(8,128)}) custom-call(s32[2]{0:T(128)S(1)} %pad_add_fusion.refs_0_, bf16[288,384]{1,0:T(8,128)(2,1)S(1)} %pad_maximum_fusion.refs_1_, bf16[288,384]{1,0:T(8,128)(2,1)S(1)} %collective-permute-done.10.refs_2_), custom_call_target="tpu_custom_call" | custom-call | flops 1000 | bytes 1000 | tf_op jit(solution)/shard_map/finish_early/pallas_call | solution.py:389
  124.4 1.3 %finish_late.1 = (f32[48,1152]{1,0:T(8,128)}, f32[48,384]{1,0:T(8,128)}, f32[3,384]{1,0:T(4,128)}) custom-call(s32[2]{0:T(128)S(1)} %pad_add_fusion.refs_0_, bf16[112,384]{1,0:T(8,128)(2,1)S(1)} %get-tuple-element.86.refs_1_, bf16[112,384]{1,0:T(8,128)(2,1)S(1)} %collective-permute-done.4.refs_2_), custom_call_target="tpu_custom_call" | custom-call | flops 1000 | bytes 1000 | tf_op jit(solution)/shard_map/finish_late/pallas_call | solution.py:389
  (51 shorter events, 6.7 us)
Async XLA Ops:
  0.6 16.9 %all-to-all-start = ((bf16[8,48,384]{2,1,0:T(8,128)(2,1)}), bf16[8,48,384]{2,1,0:T(8,128)(2,1)S(1)}, u32[]{:S(2)}, u32[]{:S(2)}) async-start(bf16[8,48,384]{2,1,0:T(8,128)(2,1)} %bitcast.41), calls=%async_computation | async-start | bytes 589824 | tf_op jit(solution)/shard_map/all_to_all | solution.py:546
  17.5 8.4 %copy-start.3 = (bf16[8,48,384]{2,1,0:T(8,128)(2,1)}, bf16[8,48,384]{2,1,0:T(8,128)(2,1)S(1)}, u32[]{:S(2)}) copy-start(bf16[8,48,384]{2,1,0:T(8,128)(2,1)S(1)} %all-to-all-done) | copy-start | bytes 884740
  21.1 12.8 %all-to-all-start.1 = ((bf16[8,48,384]{2,1,0:T(8,128)(2,1)}), bf16[8,48,384]{2,1,0:T(8,128)(2,1)S(1)}, u32[]{:S(2)}, u32[]{:S(2)}) async-start(bf16[8,48,384]{2,1,0:T(8,128)(2,1)} %bitcast.4), calls=%async_computation.1 | async-start | bytes 589824 | tf_op jit(solution)/shard_map/all_to_all | solution.py:546
  26.0 7.9 %copy-start.6 = (bf16[384,384]{1,0:T(8,128)(2,1)}, bf16[384,384]{1,0:T(8,128)(2,1)S(1)}, u32[]{:S(2)}) copy-start(bf16[384,384]{1,0:T(8,128)(2,1)S(1)} %get-tuple-element.58.refs_5_.refs_6_) | copy-start | bytes 884740
  43.2 5.6 %copy-start.8 = (bf16[384,384]{1,0:T(8,128)(2,1)}, bf16[384,384]{1,0:T(8,128)(2,1)S(1)}, u32[]{:S(2)}) copy-start(bf16[384,384]{1,0:T(8,128)(2,1)S(1)} %get-tuple-element.62.refs_1_.refs_4_) | copy-start | bytes 884740
  43.2 15.1 %collective-permute-start = (bf16[8,192,384]{2,1,0:T(8,128)(2,1)}, bf16[8,192,384]{2,1,0:T(8,128)(2,1)S(1)}, u32[]{:S(2)}, u32[]{:S(2)}) collective-permute-start(bf16[8,192,384]{2,1,0:T(8,128)(2,1)} %bitcast.8), channel_id=1, source_target_pairs={{0,1},{1,0},{2,3},{3,2},{4,5},{5,4},{6,7},{7,6},{8,9},{9,8},{10,11... | collective-permute-start | bytes 3538952 | tf_op jit(solution)/shard_map/ppermute | solution.py:446
  43.3 1.0 copy-start.7
  48.8 0.7 copy-start.10
  49.5 13.8 %all-to-all-start.2 = ((bf16[8,48,384]{2,1,0:T(8,128)(2,1)}), bf16[8,48,384]{2,1,0:T(8,128)(2,1)S(1)}, u32[]{:S(2)}, u32[]{:S(2)}) async-start(bf16[8,48,384]{2,1,0:T(8,128)(2,1)} %bitcast.36), calls=%async_computation.2 | async-start | bytes 589824 | tf_op jit(solution)/shard_map/all_to_all | solution.py:546
  58.0 15.8 %collective-permute-start.1 = (bf16[8,96,384]{2,1,0:T(8,128)(2,1)}, bf16[8,96,384]{2,1,0:T(8,128)(2,1)S(1)}, u32[]{:S(2)}, u32[]{:S(2)}) collective-permute-start(bf16[8,96,384]{2,1,0:T(8,128)(2,1)} %bitcast.12), channel_id=1, source_target_pairs={{0,1},{1,0},{2,3},{3,2},{4,5},{5,4},{6,7},{7,6},{8,9},{9,8},{10,11... | collective-permute-start | bytes 1769480 | tf_op jit(solution)/shard_map/ppermute | solution.py:446
  58.5 0.8 copy-start.9
  63.3 7.0 %copy-start.4 = (bf16[8,48,384]{2,1,0:T(8,128)(2,1)}, bf16[8,48,384]{2,1,0:T(8,128)(2,1)S(1)}, u32[]{:S(2)}) copy-start(bf16[8,48,384]{2,1,0:T(8,128)(2,1)S(1)} %all-to-all-done.2) | copy-start | bytes 884740
  63.3 14.0 %collective-permute-start.2 = (bf16[4,192,384]{2,1,0:T(8,128)(2,1)}, bf16[4,192,384]{2,1,0:T(8,128)(2,1)S(1)}, u32[]{:S(2)}, u32[]{:S(2)}) collective-permute-start(bf16[4,192,384]{2,1,0:T(8,128)(2,1)} %copy-done.9), channel_id=1, source_target_pairs={{0,2},{2,0},{4,6},{6,4},{8,10},{10,8},{12,14},{14,12},{1,3},{3,1},... | collective-permute-start | bytes 1769480 | tf_op jit(solution)/shard_map/ppermute | solution.py:480
  64.8 5.6 %copy-start.12 = (f32[3,384]{1,0:T(4,128)S(1)}, f32[3,384]{1,0:T(4,128)}, u32[]{:S(2)}) copy-start(f32[3,384]{1,0:T(4,128)} %refs_3_.1) | copy-start | bytes 13828
  70.4 7.8 %collective-permute-start.3 = (bf16[8,96,384]{2,1,0:T(8,128)(2,1)S(1)}, bf16[8,96,384]{2,1,0:T(8,128)(2,1)S(1)}, u32[]{:S(2)}, u32[]{:S(2)}) collective-permute-start(bf16[8,96,384]{2,1,0:T(8,128)(2,1)S(1)} %bitcast.38), channel_id=1, source_target_pairs={{0,1},{1,0},{2,3},{3,2},{4,5},{5,4},{6,7},{7,6},{8,9},{9,8},{10,11... | collective-permute-start | bytes 1769480 | tf_op jit(solution)/shard_map/ppermute | solution.py:446
  70.5 1.0 copy-start.5
  71.4 2.4 %copy-start = (bf16[768,384]{1,0:T(8,128)(2,1)S(1)}, bf16[768,384]{1,0:T(8,128)(2,1)}, u32[]{:S(2)}) copy-start(bf16[768,384]{1,0:T(8,128)(2,1)} %get-tuple-element.67) | copy-start | bytes 1769476
  73.8 4.4 %copy-start.13 = (f32[1,384]{1,0:T(1,128)S(1)}, f32[1,384]{1,0:T(1,128)}, u32[]{:S(2)}) copy-start(f32[1,384]{1,0:T(1,128)} %get-tuple-element.84.refs_5_) | copy-start | bytes 4612
  73.8 4.4 %copy-start.14 = (f32[1,384]{1,0:T(1,128)S(1)}, f32[1,384]{1,0:T(1,128)}, u32[]{:S(2)}) copy-start(f32[1,384]{1,0:T(1,128)} %get-tuple-element.83.refs_4_) | copy-start | bytes 4612
  73.9 0.7 copy-start.11
  77.4 0.8 copy-start.1
  79.3 41.1 %all-to-all-start.3 = ((bf16[8,160,384]{2,1,0:T(8,128)(2,1)}), bf16[8,160,384]{2,1,0:T(8,128)(2,1)}, u32[]{:S(2)}, u32[]{:S(2)}) async-start(bf16[8,160,384]{2,1,0:T(8,128)(2,1)} %pack.1), calls=%async_computation.3 | async-start | bytes 1966080 | tf_op jit(solution)/shard_map/all_to_all | solution.py:670
  84.4 17.3 %collective-permute-start.7 = (bf16[4,96,384]{2,1,0:T(8,128)(2,1)}, bf16[4,96,384]{2,1,0:T(8,128)(2,1)S(1)}, u32[]{:S(2)}, u32[]{:S(2)}) collective-permute-start(bf16[4,96,384]{2,1,0:T(8,128)(2,1)} %copy-done.11), channel_id=1, source_target_pairs={{0,2},{2,0},{4,6},{6,4},{8,10},{10,8},{12,14},{14,12},{1,3},{3,1},... | collective-permute-start | bytes 884744 | tf_op jit(solution)/shard_map/ppermute | solution.py:480
  86.4 1.1 copy-start.2
  87.6 22.3 %collective-permute-start.5 = (bf16[2,192,384]{2,1,0:T(8,128)(2,1)S(1)}, bf16[2,192,384]{2,1,0:T(8,128)(2,1)S(1)}, u32[]{:S(2)}, u32[]{:S(2)}) collective-permute-start(bf16[2,192,384]{2,1,0:T(8,128)(2,1)S(1)} %block_sum.10), channel_id=1, source_target_pairs={{0,4},{2,6},{4,0},{6,2},{8,12},{10,14},{12,8},{14,10},{1,5},{3,7},... | collective-permute-start | bytes 884744 | tf_op jit(solution)/shard_map/ppermute | solution.py:480
  101.8 11.2 %collective-permute-start.8 = (bf16[2,96,384]{2,1,0:T(8,128)(2,1)S(1)}, bf16[2,96,384]{2,1,0:T(8,128)(2,1)S(1)}, u32[]{:S(2)}, u32[]{:S(2)}) collective-permute-start(bf16[2,96,384]{2,1,0:T(8,128)(2,1)S(1)} %block_sum.13), channel_id=1, source_target_pairs={{0,4},{2,6},{4,0},{6,2},{8,12},{10,14},{12,8},{14,10},{1,5},{3,7},... | collective-permute-start | bytes 442376 | tf_op jit(solution)/shard_map/ppermute | solution.py:480
  110.0 9.5 %collective-permute-start.6 = (bf16[1,192,384]{2,1,0:T(8,128)(2,1)S(1)}, bf16[1,192,384]{2,1,0:T(8,128)(2,1)S(1)}, u32[]{:S(2)}, u32[]{:S(2)}) collective-permute-start(bf16[1,192,384]{2,1,0:T(8,128)(2,1)S(1)} %block_sum.11), channel_id=1, source_target_pairs={{0,8},{2,10},{4,12},{6,14},{8,0},{10,2},{12,4},{14,6},{1,9},{3,11}... | collective-permute-start | bytes 442376 | tf_op jit(solution)/shard_map/ppermute | solution.py:480
  113.1 7.1 %collective-permute-start.9 = (bf16[1,96,384]{2,1,0:T(8,128)(2,1)S(1)}, bf16[1,96,384]{2,1,0:T(8,128)(2,1)S(1)}, u32[]{:S(2)}, u32[]{:S(2)}) collective-permute-start(bf16[1,96,384]{2,1,0:T(8,128)(2,1)S(1)} %block_sum.14), channel_id=1, source_target_pairs={{0,8},{2,10},{4,12},{6,14},{8,0},{10,2},{12,4},{14,6},{1,9},{3,11}... | collective-permute-start | bytes 221192 | tf_op jit(solution)/shard_map/ppermute | solution.py:480
  120.3 2.6 %collective-permute-start.10 = (bf16[288,384]{1,0:T(8,128)(2,1)S(1)}, bf16[288,384]{1,0:T(8,128)(2,1)S(1)}, u32[]{:S(2)}, u32[]{:S(2)}) collective-permute-start(bf16[288,384]{1,0:T(8,128)(2,1)S(1)} %pad_maximum_fusion.refs_1_), channel_id=1, source_target_pairs={{0,1},{1,0},{2,3},{3,2},{4,5},{5,4},{6,7},{7,6},{8,9},{9,8},{10,11... | collective-permute-start | bytes 663560 | tf_op jit(solution)/shard_map/ppermute | solution.py:446
  122.4 2.1 %collective-permute-start.4 = (bf16[112,384]{1,0:T(8,128)(2,1)S(1)}, bf16[112,384]{1,0:T(8,128)(2,1)S(1)}, u32[]{:S(2)}, u32[]{:S(2)}) collective-permute-start(bf16[112,384]{1,0:T(8,128)(2,1)S(1)} %get-tuple-element.86.refs_1_), channel_id=1, source_target_pairs={{0,1},{1,0},{2,3},{3,2},{4,5},{5,4},{6,7},{7,6},{8,9},{9,8},{10,11... | collective-permute-start | bytes 258056 | tf_op jit(solution)/shard_map/ppermute | solution.py:446
